TPU v7x, 256 devices: a whole 4x4x8 slice. The times are simulated.
256 devices in a mesh: inst: 32 (over x, y, core), tp: 8 (over z).
Axes of the slice: x: 4, y: 4, z: 8, core: 2. Of those that a mesh axis runs over, the one named last changes fastest.
Arguments:
- queries: bfloat16 [256, 4, 64, 128], P('inst', None, 'tp'), may hold values from -32 to 32
- new_kv: bfloat16 [256, 2, 4, 8, 128], P('inst', None, None, 'tp'), may hold values from -6 to 6
- kv_cache: bfloat16 [2048, 2, 8, 64, 128], P('inst', None, 'tp'), may hold values from -32 to 32
- block_owner: int32 [2048], P('inst'), may hold values from 0 to 255
- block_fill: int32 [2048], P('inst'), may hold values from 0 to 64, as said below
- move_slot: int32 [768], P('inst'), may hold values from 0 to 63, as said below
- move_target: int32 [768, 1], P('inst'), may hold values from 0 to 31; in each aligned block of 24 rows (0 to 23, 24 to 47, ...) at most 2 rows name the same one
- out_weight: bfloat16 [8192, 4096], P('tp'), may hold values from -0.0625 to 0.0625
Outputs:
- attention_out: bfloat16 [1024, 4096], P('inst', 'tp')
- moved_blocks: bfloat16 [2048, 2, 8, 64, 128], P('inst', None, 'tp')
Inputs may be any that keep to these rules, and one draw needn't show every extreme that they name: `block_fill`: 0 marks an empty slot; the first slot of every instance is full. `move_slot`: the 24 entries of one instance name distinct slots of that instance. `move_target`: among one instance's 24 entries no destination is named more than 2 times, a bound that some block reaches.
All inputs are finite; a program needn't handle non-finite values.
Results may differ from a plain program's by a relative error of at most 0.019.
Values may be sent and summed in bfloat16 or wider, within the bound.
A program may use at most 128 MiB of HBM per device.

v0:
```python
import jax
import jax.numpy as jnp
from jax import lax
from jax.sharding import PartitionSpec as P

CAPACITY = 2


MASKED = -1e30


def partial_softmax(query_rows, key_rows, value_rows, usable):
    factor = query_rows.shape[-1] ** (-0.5)
    scores = (
        jnp.einsum("ntkgd,nksd->nktgs", query_rows, key_rows, preferred_element_type=jnp.float32)
        * factor
    )
    highest = jnp.max(jnp.where(usable, scores, MASKED), axis=-1)
    exp_scores = jnp.where(usable, jnp.exp(scores - highest[..., None]), 0.0)
    row_total = jnp.sum(exp_scores, axis=-1)
    weighted = jnp.einsum(
        "nktgs,nksd->nktgd",
        exp_scores.astype(jnp.bfloat16),
        value_rows,
        preferred_element_type=jnp.float32,
    )
    return (highest, row_total, weighted)


def per_request(owners, highest, row_total, weighted, requests):
    slot_count = owners.shape[0]
    flat_high = highest.reshape(slot_count, -1)
    flat_total = row_total.reshape(slot_count, -1)
    flat_value = weighted.reshape(slot_count, flat_high.shape[1], -1)
    member = owners[None, :] == jnp.arange(requests, dtype=jnp.int32)[:, None]
    local_high = jnp.max(jnp.where(member[:, :, None], flat_high[None], MASKED), axis=1)
    shares = jnp.where(member[:, :, None], jnp.exp(flat_high[None] - local_high[:, None]), 0.0)
    summed = jnp.einsum("rnf,nfd->rfd", shares, flat_value, precision=lax.Precision.HIGHEST)
    totals = jnp.sum(shares * flat_total[None], axis=1)
    return (local_high, totals, summed)


def shards(queries, new_kv, kv_cache, block_owner, block_fill, move_slot, move_target, out_weight):
    instances = lax.axis_size("inst")
    req_local = queries.shape[0]
    drafts = queries.shape[1]
    head_local = queries.shape[2]
    head_dim = queries.shape[3]
    slot_count = kv_cache.shape[0]
    kv_local = kv_cache.shape[2]
    block_rows = kv_cache.shape[3]
    group_size = head_local // kv_local
    requests = req_local * instances
    move_count = move_slot.shape[0]
    target = move_target[:, 0]
    entries = jnp.arange(move_count, dtype=jnp.int32)
    earlier = (target[None, :] == target[:, None]) & (entries[None, :] < entries[:, None])
    position = target * CAPACITY + jnp.sum(earlier, axis=1)
    matched = position[None, :] == jnp.arange(instances * CAPACITY, dtype=jnp.int32)[:, None]
    present = jnp.any(matched, axis=1)
    chosen = jnp.sum(jnp.where(matched, move_slot[None, :], 0), axis=1)
    send_blocks = jnp.where(
        present[:, None, None, None, None], kv_cache[chosen], jnp.zeros((), jnp.bfloat16)
    )
    all_queries = lax.all_gather(queries, "inst", axis=0, tiled=True)
    send_owner = jnp.where(present, block_owner[chosen], 0)
    send_fill = jnp.where(present, block_fill[chosen], 0)
    moved_blocks, got_owner, got_fill = (
        lax.all_to_all(send_blocks, "inst", split_axis=0, concat_axis=0, tiled=True),
        lax.all_to_all(send_owner, "inst", split_axis=0, concat_axis=0, tiled=True),
        lax.all_to_all(send_fill, "inst", split_axis=0, concat_axis=0, tiled=True),
    )
    leaving = jnp.any(
        move_slot[None, :] == jnp.arange(slot_count, dtype=jnp.int32)[:, None], axis=1
    )
    owners = jnp.concatenate([block_owner, got_owner])
    fill_rows = jnp.concatenate([jnp.where(leaving, 0, block_fill), got_fill])
    resident = jnp.concatenate([kv_cache, moved_blocks])
    query_rows = all_queries[owners].reshape(
        owners.shape[0], drafts, kv_local, group_size, head_dim
    )
    usable = (
        jnp.arange(block_rows, dtype=jnp.int32)[None, None, None, None, :]
        < fill_rows[:, None, None, None, None]
    )
    highest, row_total, weighted = partial_softmax(
        query_rows, resident[:, 0], resident[:, 1], usable
    )
    local_high, totals, summed = per_request(owners, highest, row_total, weighted, requests)
    own_rows = queries.reshape(req_local, drafts, kv_local, group_size, head_dim)
    draft_keys = jnp.transpose(new_kv[:, 0], (0, 2, 1, 3))
    draft_values = jnp.transpose(new_kv[:, 1], (0, 2, 1, 3))
    causal = (
        jnp.arange(drafts)[None, None, None, None, :]
        <= jnp.arange(drafts)[None, None, :, None, None]
    )
    draft_high, draft_total, draft_weighted = partial_softmax(
        own_rows, draft_keys, draft_values, causal
    )
    draft_high = draft_high.reshape(req_local, -1)
    draft_total = draft_total.reshape(req_local, -1)
    draft_weighted = draft_weighted.reshape(req_local, draft_high.shape[1], head_dim)
    got_high, got_total, got_summed = (
        lax.all_to_all(local_high[:, None], "inst", split_axis=0, concat_axis=1, tiled=True),
        lax.all_to_all(totals[:, None], "inst", split_axis=0, concat_axis=1, tiled=True),
        lax.all_to_all(summed[:, None], "inst", split_axis=0, concat_axis=1, tiled=True),
    )
    highest_all = jnp.maximum(jnp.max(got_high, axis=1), draft_high)
    shares = jnp.exp(got_high - highest_all[:, None])
    numerator = jnp.sum(shares[..., None] * got_summed, axis=1)
    denominator = jnp.sum(shares * got_total, axis=1)
    draft_part = jnp.exp(draft_high - highest_all)
    numerator = numerator + draft_part[..., None] * draft_weighted
    denominator = denominator + draft_part * draft_total
    attention = (numerator / denominator[..., None]).reshape(
        req_local, kv_local, drafts, group_size, head_dim
    )
    attention = (
        jnp.transpose(attention, (0, 2, 1, 3, 4))
        .reshape(req_local * drafts, head_local * head_dim)
        .astype(jnp.bfloat16)
    )
    projected = jnp.dot(attention, out_weight, preferred_element_type=jnp.float32)
    attention_out = lax.psum_scatter(
        projected.astype(jnp.bfloat16), "tp", scatter_dimension=1, tiled=True
    )
    return (attention_out, moved_blocks)


def solution(mesh):
    placed = (
        P("inst", None, "tp", None),
        P("inst", None, None, "tp", None),
        P("inst", None, "tp", None, None),
        P("inst"),
        P("inst"),
        P("inst"),
        P("inst", None),
        P("tp", None),
    )
    return jax.shard_map(
        shards,
        mesh=mesh,
        in_specs=placed,
        out_specs=(P("inst", "tp"), P("inst", None, "tp", None, None)),
        check_vma=False,
    )
```

profile of v0, /device:TPU:2, one launch (start us, length us, event | category | flops | bytes accessed | tf_op | source)
XLA Modules:
  0.0 240.1 jit_solution(15049933936009642049)
XLA Ops:
  13.9 7.6 %all-to-all-start.1 = ((s32[32,2,1]{1,2,0:T(1,128)}), s32[32,2,1]{1,2,0:T(1,128)S(1)}, u32[]{:S(2)}, u32[]{:S(2)}) async-start(s32[32,2,1]{1,2,0:T(1,128)} %bitcast.4), calls=%async_computation.1 | async-start | bytes 32768 | tf_op jit(solution)/shard_map/all_to_all | solution.py:71
  22.3 2.5 %gather_fusion.3 = bf16[64,2,64,128]{3,2,1,0:T(8,128)(2,1)S(1)} fusion(bf16[64,2,64,128]{3,2,1,0:T(8,128)(2,1)} %bitcast.103, s32[1024]{0:T(1024)S(1)} %pad_clamp_fusion.1), kind=kCustom, calls=%fused_computation.3 | custom fusion | bytes 4194560 | tf_op jit(solution)/shard_map/gather | solution.py:63
  24.8 2.9 %all-to-all-done.1 = s32[32,2,1]{1,2,0:T(1,128)S(1)} async-done(((s32[32,2,1]{1,2,0:T(1,128)}), s32[32,2,1]{1,2,0:T(1,128)S(1)}, u32[]{:S(2)}, u32[]{:S(2)}) %all-to-all-start.1) | async-done | bytes 288 | tf_op jit(solution)/shard_map/all_to_all | solution.py:71
  27.7 5.0 %all-to-all-start = ((s32[32,2,1]{1,2,0:T(1,128)}), s32[32,2,1]{1,2,0:T(1,128)S(1)}, u32[]{:S(2)}, u32[]{:S(2)}) async-start(s32[32,2,1]{1,2,0:T(1,128)} %bitcast.3), calls=%async_computation | async-start | bytes 32768 | tf_op jit(solution)/shard_map/all_to_all | solution.py:70
  32.6 1.5 fusion.4
  34.2 4.7 %all-to-all-done = s32[32,2,1]{1,2,0:T(1,128)S(1)} async-done(((s32[32,2,1]{1,2,0:T(1,128)}), s32[32,2,1]{1,2,0:T(1,128)S(1)}, u32[]{:S(2)}, u32[]{:S(2)}) %all-to-all-start) | async-done | bytes 288 | tf_op jit(solution)/shard_map/all_to_all | solution.py:70
  38.9 5.1 %all-to-all-start.2 = ((bf16[64,2,1,64,128]{4,3,2,1,0:T(8,128)(2,1)}), bf16[64,2,1,64,128]{4,3,2,1,0:T(8,128)(2,1)S(1)}, u32[]{:S(2)}, u32[]{:S(2)}) async-start(bf16[64,2,1,64,128]{4,3,2,1,0:T(8,128)(2,1)} %fusion.4), calls=%async_computation.2 | async-start | bytes 4194304 | tf_op jit(solution)/shard_map/all_to_all | solution.py:69
  44.1 3.3 %constant_dynamic-update-slice_fusion.1 = bf16[128,2,1,64,128]{4,3,2,1,0:T(8,128)(2,1)} fusion(bf16[64,2,1,64,128]{4,3,2,1,0:T(8,128)(2,1)} %param.10), kind=kLoop, calls=%fused_computation.63 | loop fusion | bytes 4194304
  50.0 23.7 %all-to-all-done.2 = bf16[64,2,1,64,128]{4,3,2,1,0:T(8,128)(2,1)S(1)} async-done(((bf16[64,2,1,64,128]{4,3,2,1,0:T(8,128)(2,1)}), bf16[64,2,1,64,128]{4,3,2,1,0:T(8,128)(2,1)S(1)}, u32[]{:S(2)}, u32[]{:S(2)}) %all-to-all-start.2) | async-done | bytes 2097184 | tf_op jit(solution)/shard_map/all_to_all | solution.py:69
  73.7 1.6 constant_dynamic-update-slice_fusion
  76.1 2.3 gather_fusion.2
  78.5 4.2 %select_reduce_fusion.1 = (f32[128,4,8]{2,1,0:T(4,128)S(1)}, f32[128,4,8,64]{3,2,1,0:T(8,128)}) fusion(pred[128,64]{1,0:T(8,128)(4,1)S(1)} %iota_compare_fusion.1, bf16[128,4,8,128]{3,2,1,0:T(8,128)(2,1)S(1)} %gather_fusion.2, bf16[128,2,1,64,128]{4,3,2,1,0:T(8,128)(2,1)} %constant_dynamic-update-slice_fusion), kind=kOutput, calls=%fused_computation.22 | convolution fusion | flops 67891200 | bytes 4218880 | tf_op jit(solution)/shard_map/ntkgd,nksd->nktgs/dot_general | solution.py:15
  82.8 2.6 %fusion.11 = f32[128,4,8]{2,1,0:T(4,128)S(1)} fusion(f32[128,4,8,64]{3,2,1,0:T(8,128)} %get-tuple-element.13, f32[128,4,8]{2,1,0:T(4,128)S(1)} %get-tuple-element.12, pred[128,64]{1,0:T(8,128)(4,1)S(1)} %iota_compare_fusion.1), kind=kLoop, calls=%fused_computation.25 | loop fusion | flops 1044480 | bytes 1089536 | tf_op jit(solution)/shard_map/reduce_sum | solution.py:20
  86.7 2.4 %multiply_reduce_fusion = f32[256,32]{0,1:T(8,128)S(1)} fusion(f32[128,32]{0,1:T(8,128)S(1)} %bitcast.114, f32[256,32]{0,1:T(8,128)S(1)} %select_reduce_fusion, f32[128,32]{0,1:T(8,128)S(1)} %bitcast.110, pred[256,128]{1,0:T(8,128)(4,1)S(1)} %iota_compare_fusion), kind=kLoop, calls=%fused_computation.5 | loop fusion | flops 4186112 | bytes 131072 | tf_op jit(solution)/shard_map/reduce_sum | solution.py:39
  91.2 6.2 %all-to-all-start.5 = ((f32[32,1,256]{2,1,0:T(1,128)}), f32[32,1,256]{2,1,0:T(1,128)S(1)}, u32[]{:S(2)}, u32[]{:S(2)}) async-start(f32[32,1,256]{2,1,0:T(1,128)} %reshape.410), calls=%async_computation.5 | async-start | bytes 65536 | tf_op jit(solution)/shard_map/all_to_all | solution.py:105
  97.4 4.4 %fusion.10 = f32[128,32,128]{2,1,0:T(8,128)} fusion(bf16[128,2,1,64,128]{4,3,2,1,0:T(8,128)(2,1)} %constant_dynamic-update-slice_fusion, f32[128,4,8,64]{3,2,1,0:T(8,128)} %get-tuple-element.13, f32[128,4,8]{2,1,0:T(4,128)S(1)} %get-tuple-element.12, pred[128,64]{1,0:T(8,128)(4,1)S(1)} %iota_compare_fusion.1), kind=kOutput, calls=%fused_computation.24 | convolution fusion | flops 68157440 | bytes 6316032 | tf_op jit(solution)/shard_map/nktgs,nksd->nktgd/dot_general | solution.py:21
  103.6 7.0 %all-to-all-start.3 = ((f32[32,1,256]{2,1,0:T(1,128)}), f32[32,1,256]{2,1,0:T(1,128)S(1)}, u32[]{:S(2)}, u32[]{:S(2)}) async-start(f32[32,1,256]{2,1,0:T(1,128)} %reshape.408), calls=%async_computation.3 | async-start | bytes 65536 | tf_op jit(solution)/shard_map/all_to_all | solution.py:104
  110.7 8.2 %fusion.1 = f32[256,1,32,128]{0,3,2,1:T(8,128)} fusion(f32[128,32,128]{2,1,0:T(8,128)} %fusion.10, f32[256,32]{0,1:T(8,128)S(1)} %select_reduce_fusion, f32[128,32]{0,1:T(8,128)S(1)} %bitcast.111, pred[256,128]{1,0:T(8,128)(4,1)S(1)} %iota_compare_fusion), kind=kOutput, calls=%fused_computation.10 | convolution fusion | flops 1612709888 | bytes 6373376 | tf_op jit(solution)/shard_map/rnf,nfd->rfd/dot_general | solution.py:38
  118.8 5.5 %copy.61 = f32[256,1,32,128]{3,2,1,0:T(8,128)} copy(f32[256,1,32,128]{0,3,2,1:T(8,128)} %fusion.1) | data formatting | bytes 8388608 | tf_op jit(solution)/shard_map/broadcast_in_dim | solution.py:106
  124.3 7.6 %all-to-all-start.4 = ((f32[256,1,32,128]{3,2,1,0:T(8,128)}), f32[256,1,32,128]{3,2,1,0:T(8,128)}, u32[]{:S(2)}, u32[]{:S(2)}) async-start(f32[256,1,32,128]{3,2,1,0:T(8,128)} %copy.61), calls=%async_computation.4 | async-start | bytes 8388608 | tf_op jit(solution)/shard_map/all_to_all | solution.py:106
  135.3 46.8 %all-to-all-done.4 = f32[256,1,32,128]{3,2,1,0:T(8,128)} async-done(((f32[256,1,32,128]{3,2,1,0:T(8,128)}), f32[256,1,32,128]{3,2,1,0:T(8,128)}, u32[]{:S(2)}, u32[]{:S(2)}) %all-to-all-start.4) | async-done | bytes 4194336 | tf_op jit(solution)/shard_map/all_to_all | solution.py:106
  182.2 2.8 %multiply_reduce_fusion.1 = f32[8,32,128]{2,1,0:T(8,128)S(1)} fusion(f32[8,32,32,128]{3,2,0,1:T(8,128)} %bitcast.30, f32[8,32,32]{2,0,1:T(8,128)S(1)} %get-tuple-element.9), kind=kLoop, calls=%fused_computation.6 | loop fusion | flops 2064384 | bytes 4358144 | tf_op jit(solution)/shard_map/reduce_sum | solution.py:110
  185.1 5.6 %convolution_convert_fusion = bf16[32,4096]{1,0:T(8,128)(2,1)} fusion(bf16[1024,4096]{1,0:T(8,128)(2,1)} %param.15, f32[32,1024]{1,0:T(8,128)S(1)} %div.12, f32[32,1024]{1,0:T(8,128)S(1)} %reduce_sum.71, f32[32,1024]{1,0:T(8,128)S(1)} %mul.68, f32[4,8,8,128]{3,2,1,0:T(8,128)S(1)} %bitcast.106), kind=kOutput, calls=%fused_computation.4 | convolution fusion | flops 268697600 | bytes 9175040 | tf_op jit(solution)/shard_map/dot_general | solution.py:123
  190.7 41.3 %reduce-scatter.2.cloned.1.call-done = bf16[32,512]{1,0:T(8,128)(2,1)} async-done(((bf16[32,4096]{1,0:T(8,128)(2,1)}), bf16[32,512]{1,0:T(8,128)(2,1)}) %reduce-scatter.2.cloned.1.call-update) | async-done | bytes 32784 | tf_op jit(solution)/shard_map/reduce_scatter | solution.py:124
  (72 shorter events, 20.8 us)
Async XLA Ops:
  7.2 69.0 %all-gather.2.cloned.1.call-start = ((), (), s32[]{:S(2)}) async-start(), calls=%async_computation.7 | async-start | bytes 2162688 | tf_op jit(solution)/shard_map/all_gather | solution.py:65
  13.9 13.7 %all-to-all-start.1 = ((s32[32,2,1]{1,2,0:T(1,128)}), s32[32,2,1]{1,2,0:T(1,128)S(1)}, u32[]{:S(2)}, u32[]{:S(2)}) async-start(s32[32,2,1]{1,2,0:T(1,128)} %bitcast.4), calls=%async_computation.1 | async-start | bytes 32768 | tf_op jit(solution)/shard_map/all_to_all | solution.py:71
  27.7 11.2 %all-to-all-start = ((s32[32,2,1]{1,2,0:T(1,128)}), s32[32,2,1]{1,2,0:T(1,128)S(1)}, u32[]{:S(2)}, u32[]{:S(2)}) async-start(s32[32,2,1]{1,2,0:T(1,128)} %bitcast.3), calls=%async_computation | async-start | bytes 32768 | tf_op jit(solution)/shard_map/all_to_all | solution.py:70
  34.2 9.9 %copy-start.4 = (s32[24]{0:T(128)S(1)}, s32[24]{0:T(128)}, u32[]{:S(2)}) copy-start(s32[24]{0:T(128)} %param.13) | copy-start | bytes 292
  38.9 34.9 %all-to-all-start.2 = ((bf16[64,2,1,64,128]{4,3,2,1,0:T(8,128)(2,1)}), bf16[64,2,1,64,128]{4,3,2,1,0:T(8,128)(2,1)S(1)}, u32[]{:S(2)}, u32[]{:S(2)}) async-start(bf16[64,2,1,64,128]{4,3,2,1,0:T(8,128)(2,1)} %fusion.4), calls=%async_computation.2 | async-start | bytes 4194304 | tf_op jit(solution)/shard_map/all_to_all | solution.py:69
  44.1 3.3 %copy-start = (s32[64]{0:T(128)S(1)}, s32[64]{0:T(128)}, u32[]{:S(2)}) copy-start(s32[64]{0:T(128)} %param.12) | copy-start | bytes 772
  44.1 5.5 %copy-start.1 = (s32[64]{0:T(128)S(1)}, s32[64]{0:T(128)}, u32[]{:S(2)}) copy-start(s32[64]{0:T(128)} %param.11) | copy-start | bytes 772
  91.2 12.4 %all-to-all-start.5 = ((f32[32,1,256]{2,1,0:T(1,128)}), f32[32,1,256]{2,1,0:T(1,128)S(1)}, u32[]{:S(2)}, u32[]{:S(2)}) async-start(f32[32,1,256]{2,1,0:T(1,128)} %reshape.410), calls=%async_computation.5 | async-start | bytes 65536 | tf_op jit(solution)/shard_map/all_to_all | solution.py:105
  103.6 20.7 %all-to-all-start.3 = ((f32[32,1,256]{2,1,0:T(1,128)}), f32[32,1,256]{2,1,0:T(1,128)S(1)}, u32[]{:S(2)}, u32[]{:S(2)}) async-start(f32[32,1,256]{2,1,0:T(1,128)} %reshape.408), calls=%async_computation.3 | async-start | bytes 65536 | tf_op jit(solution)/shard_map/all_to_all | solution.py:104
  124.3 7.7 %copy-start.2 = (bf16[8,4,8,128]{3,2,1,0:T(8,128)(2,1)S(1)}, bf16[8,4,8,128]{3,2,1,0:T(8,128)(2,1)}, u32[]{:S(2)}) copy-start(bf16[8,4,8,128]{3,2,1,0:T(8,128)(2,1)} %param.8) | copy-start | bytes 196612
  124.3 7.7 %copy-start.3 = (bf16[8,2,4,1,128]{4,2,3,1,0:T(4,128)(2,1)S(1)}, bf16[8,2,4,1,128]{4,2,3,1,0:T(4,128)(2,1)}, u32[]{:S(2)}) copy-start(bf16[8,2,4,1,128]{4,2,3,1,0:T(4,128)(2,1)} %param.9) | copy-start | bytes 49156
  124.3 57.8 %all-to-all-start.4 = ((f32[256,1,32,128]{3,2,1,0:T(8,128)}), f32[256,1,32,128]{3,2,1,0:T(8,128)}, u32[]{:S(2)}, u32[]{:S(2)}) async-start(f32[256,1,32,128]{3,2,1,0:T(8,128)} %copy.61), calls=%async_computation.4 | async-start | bytes 8388608 | tf_op jit(solution)/shard_map/all_to_all | solution.py:106
  131.9 100.0 %reduce-scatter.2.cloned.1.call-start = ((), (), s32[]{:S(2)}) async-start(), calls=%async_computation.8 | async-start | bytes 294912 | tf_op jit(solution)/shard_map/reduce_scatter | solution.py:124
Sparse Core Ops, SparseCore 0:
  10.6 65.5 all-gather.1
  190.8 41.1 reduce-scatter.1
where the time goes:
time: 241 us; the launch traced here: 240 us
  waiting for transfers between devices  121 us (50%)
  starting transfers between devices  38.6 us (16%)
  local copies, waits for them, and re-layouts  25 us (10%)
  matrix products  23.1 us (10%)
  other arithmetic  17.9 us (7%)
  between operations  14.3 us (6%)
    all_to_all x1, waiting for transfers between devices, shards(): lax.all_to_all(summed[:, None], 'inst', split_axis=0, concat_axis=1, tile...  46.8 us
    reduce_scatter x1, waiting for transfers between devices, shards(): lax.psum_scatter(projected.astype(jnp.bfloat16), 'tp', scatter_dimension=...  41.3 us
    all_to_all x1, waiting for transfers between devices, shards(): lax.all_to_all(send_blocks, 'inst', split_axis=0, concat_axis=0, tiled=True)  23.7 us
    dot_general x1, matrix products, per_request(): jnp.einsum('rnf,nfd->rfd', shares, flat_value, precision=lax.Precision.HI...  8.17 us
    all_to_all x1, starting transfers between devices, shards(): lax.all_to_all(send_fill, 'inst', split_axis=0, concat_axis=0, tiled=True)  7.62 us
    all_to_all x1, starting transfers between devices, shards(): lax.all_to_all(summed[:, None], 'inst', split_axis=0, concat_axis=1, tile...  7.58 us
    all_to_all x1, starting transfers between devices, shards(): lax.all_to_all(local_high[:, None], 'inst', split_axis=0, concat_axis=1,...  7.05 us
    unnamed x18, local copies, waits for them, and re-layouts  6.72 us
  transfers between devices with their start and end apart: 8, of which 7 were waited for; matrix products, arithmetic and copies ran while one was open for 17% of the time, Pallas kernels for 0%

commit v1 on v0

v1 whole, which is shorter than its diff:
```python
import functools

import jax
import jax.numpy as jnp
from jax import lax
from jax.experimental import pallas as pl
from jax.experimental.pallas import tpu as pltpu
from jax.sharding import PartitionSpec as P

MESH = pl.DeviceIdType.MESH
MASKED = -1e30
CAPACITY = 2
F32, BF16, I32 = jnp.float32, jnp.bfloat16, jnp.int32

INSTS = 32
CHIPS = 16
TPS = 8
SLOTS = 64
ROWS = 64
DIM = 128
HEADS = 8
DRAFTS = 4
LINES = DRAFTS * HEADS
REQ = 8
REQS = INSTS * REQ
GROUPS = SLOTS // 4
TILES = LINES // 2
COLS = 512
MOVES = 24
EARLY = 0


def nt_dot(a, b):
    return lax.dot_general(a, b, (((1,), (1,)), ((), ())), preferred_element_type=F32)


def tile_lines(tile):
    t, g = 2 * (tile // HEADS), tile % HEADS
    return t * HEADS + g, (t + 1) * HEADS + g


def spread(weights, tile):
    first, second = tile_lines(tile)
    return jnp.concatenate(
        [
            jnp.broadcast_to(weights[:, first : first + 1], (REQ, DIM)),
            jnp.broadcast_to(weights[:, second : second + 1], (REQ, DIM)),
        ],
        axis=0,
    )


def kernel(
    q, nkv, kv_hbm, owner, fill, slot_col, target_col, target_row, w_hbm,
    out, moved,
    kv, w, pick, pick_s, msend, qall, dkv, dval, dmax, dsum,
    score, smax, ssum, reqmax, reqsum, val, pay, aux, epay, eaux, cpay, caux,
    rpay, raux, ew, acc, att, zsend, zrecv, zout,
    load_sem, own_sem, ag_s, ag_r, sib_s, sib_r, mig_s, mig_r, e_s, e_r,
    rs_s, rs_r, ra_s, ra_r, z_s, z_r,
):
    me, tp = lax.axis_index("inst"), lax.axis_index("tp")
    core = lax.rem(me, 2)
    chip = me // 2
    sibling = me ^ 1

    def remote(src, dst, send, recv, inst, z):
        return pltpu.make_async_remote_copy(
            src_ref=src, dst_ref=dst, send_sem=send, recv_sem=recv,
            device_id=(inst, z), device_id_type=MESH,
        )

    barrier = pltpu.get_barrier_semaphore()

    @pl.loop(1, INSTS)
    def _(k):
        pl.semaphore_signal(barrier, inc=1, device_id=(me ^ k, tp), device_id_type=MESH)

    @pl.loop(1, TPS)
    def _(k):
        pl.semaphore_signal(barrier, inc=1, device_id=(me, tp ^ k), device_id_type=MESH)

    kv_load = pltpu.make_async_copy(kv_hbm, kv.at[pl.ds(0, SLOTS)], load_sem.at[0])
    kv_load.start()
    w_load = pltpu.make_async_copy(w_hbm, w, load_sem.at[1])
    w_load.start()

    kv[SLOTS] = jnp.zeros((2, ROWS, DIM), BF16)
    entry_row = lax.broadcasted_iota(I32, (MOVES, MOVES), 1)
    entry_col = lax.broadcasted_iota(I32, (MOVES, MOVES), 0)
    earlier = (target_row[...] == target_col[...]) & (entry_row < entry_col)
    position = target_col[...] * CAPACITY + jnp.sum(earlier.astype(I32), axis=1, keepdims=True)
    matched = position == lax.broadcasted_iota(I32, (MOVES, DIM), 1)
    chosen = SLOTS + jnp.sum(
        jnp.where(matched, slot_col[...] - SLOTS, 0), axis=0, keepdims=True
    )
    pick[...] = jnp.broadcast_to(chosen, (8, DIM))
    pick_load = pltpu.make_async_copy(pick, pick_s, load_sem.at[2])
    pick_load.start()

    dkv[...] = jnp.zeros(dkv.shape, F32)
    dkv[:, :, 0:DRAFTS, :] = nkv[...].astype(F32)
    lane = lax.broadcasted_iota(I32, (1, DIM), 1)
    lane_group = lane // LINES

    def by_group(parts):
        return jnp.where(
            lane_group == 0,
            parts[0],
            jnp.where(lane_group == 1, parts[1], jnp.where(lane_group == 2, parts[2], parts[3])),
        )

    for half in range(REQ // 4):
        queries = q[4 * half : 4 * half + 4].reshape(4 * LINES, DIM)
        keys = dkv[4 * half : 4 * half + 4, 0].reshape(4 * 8, DIM).astype(BF16)
        full = nt_dot(keys, queries)
        scores = by_group([full[8 * i : 8 * i + 8] for i in range(4)]) * (DIM**-0.5)
        u = lax.broadcasted_iota(I32, (8, DIM), 0)
        t = lax.rem(lax.broadcasted_iota(I32, (8, DIM), 1), LINES) // HEADS
        causal = u <= t
        high = jnp.max(jnp.where(causal, scores, MASKED), axis=0, keepdims=True)
        probs = jnp.where(causal, jnp.exp(scores - high), 0.0)
        total = jnp.sum(probs, axis=0, keepdims=True)
        turned = jnp.transpose(probs).astype(BF16)
        for i in range(4):
            r = 4 * half + i
            dmax[r : r + 1, :] = high if i == 0 else pltpu.roll(high, DIM - i * LINES, 1)
            dsum[r : r + 1, :] = total if i == 0 else pltpu.roll(total, DIM - i * LINES, 1)
            dval[r * LINES : (r + 1) * LINES, :] = jnp.dot(
                turned[i * LINES : (i + 1) * LINES],
                dkv[r, 1].astype(BF16),
                preferred_element_type=F32,
            )

    qall[pl.ds(me * REQ, REQ)] = q[...]
    pl.semaphore_wait(barrier, INSTS - 1 + TPS - 1)

    def gather_in(k):
        return remote(
            q, qall.at[pl.ds(me * REQ, REQ)], ag_s.at[k], ag_r.at[k], me ^ (2 * k), tp
        )

    def gather_on(k):
        rows = pl.ds((me ^ (2 * k)) * REQ, REQ)
        return remote(qall.at[rows], qall.at[rows], sib_s.at[k], sib_r.at[k], sibling, tp)

    gather_on(0).start()

    @pl.loop(1, CHIPS)
    def _(k):
        gather_in(k).start()

    kv_load.wait()
    pick_load.wait()

    @pl.loop(0, SLOTS)
    def _(p):
        msend[p] = kv[pick_s[0, p]]

    own = pltpu.make_async_copy(
        msend.at[pl.ds(CAPACITY * me, CAPACITY)],
        moved.at[pl.ds(CAPACITY * me, CAPACITY)],
        own_sem,
    )
    own.start()

    def migrate(k):
        return remote(
            msend.at[pl.ds(CAPACITY * (me ^ k), CAPACITY)],
            moved.at[pl.ds(CAPACITY * me, CAPACITY)],
            mig_s.at[k], mig_r.at[k], me ^ k, tp,
        )

    @pl.loop(1, CHIPS)
    def _(k):
        gather_in(k).wait_recv()
        gather_on(k).start()

    @pl.loop(1, 1 + EARLY)
    def _(k):
        migrate(k).start()

    @pl.loop(0, CHIPS)
    def _(k):
        gather_on(k).wait_recv()

    row_of = lax.broadcasted_iota(I32, (ROWS, DIM), 0)

    def usable(g):
        return row_of < by_group([fill[4 * g + i] for i in range(4)])

    @pl.loop(0, GROUPS)
    def _(g):
        queries = jnp.concatenate([qall[owner[4 * g + i]] for i in range(4)], axis=0)
        keys = kv[pl.ds(4 * g, 4), 0].reshape(4 * ROWS, DIM)
        full = nt_dot(keys, queries)
        scores = by_group([full[ROWS * i : ROWS * (i + 1)] for i in range(4)]) * (DIM**-0.5)
        scores = jnp.where(usable(g), scores, MASKED)
        score[g] = scores
        smax[pl.ds(g, 1), :] = jnp.max(scores, axis=0, keepdims=True)

    row = lax.broadcasted_iota(I32, (REQS, DIM), 0)
    request = (row % (REQS // 2)) // REQ * (2 * REQ) + row // (REQS // 2) * REQ + row % REQ

    def owners(g):
        return by_group([owner[4 * g + i] for i in range(4)])

    def all_groups(x, f):
        x = f(x, pltpu.roll(x, 2 * LINES, 1))
        return f(x, pltpu.roll(x, LINES, 1))

    reqmax[...] = jnp.full(reqmax.shape, MASKED, F32)

    @pl.loop(0, GROUPS)
    def _(g):
        reqmax[...] = jnp.where(
            request == owners(g), jnp.maximum(reqmax[...], smax[pl.ds(g, 1), :]), reqmax[...]
        )

    reqmax[...] = all_groups(reqmax[...], jnp.maximum)

    @pl.loop(0, GROUPS)
    def _(g):
        highs = []
        for i in range(4):
            o = owner[4 * g + i]
            at = lax.rem(o // REQ, 2) * (REQS // 2) + o // (2 * REQ) * REQ + lax.rem(o, REQ)
            highs.append(reqmax[pl.ds(at, 1), :])
        probs = jnp.where(usable(g), jnp.exp(score[g] - by_group(highs)), 0.0)
        ssum[pl.ds(g, 1), :] = jnp.sum(probs, axis=0, keepdims=True)
        turned = jnp.transpose(probs).astype(BF16)
        for i in range(4):
            val[pl.ds((4 * g + i) * LINES, LINES), :] = jnp.dot(
                turned[i * LINES : (i + 1) * LINES],
                kv[4 * g + i, 1],
                preferred_element_type=F32,
            )

    reqsum[...] = jnp.zeros(reqsum.shape, F32)

    @pl.loop(0, GROUPS)
    def _(g):
        reqsum[...] += jnp.where(request == owners(g), ssum[pl.ds(g, 1), :], 0.0)

    reqsum[...] = all_groups(reqsum[...], jnp.add)
    aux[...] = jnp.where(lane < LINES, reqmax[...], reqsum[...]).reshape(aux.shape)

    owner_lane = lax.broadcasted_iota(I32, (1, SLOTS), 1)

    def owner_step(b, x):
        return jnp.where(owner_lane == b, owner[b], x)

    owner_row = lax.fori_loop(0, SLOTS, owner_step, jnp.zeros((1, SLOTS), I32))
    half_row = lax.broadcasted_iota(I32, (REQS // 2, SLOTS), 0)

    def sum_slots(home_core):
        ids = half_row // REQ * (2 * REQ) + home_core * REQ + half_row % REQ
        member = (ids == owner_row).astype(F32).astype(BF16)

        @pl.loop(0, TILES)
        def _(tile):
            first = 2 * HEADS * (tile // HEADS) + lax.rem(tile, HEADS)
            lines = jnp.concatenate(
                [
                    val[pl.ds(first, SLOTS, stride=LINES), :],
                    val[pl.ds(first + HEADS, SLOTS, stride=LINES), :],
                ],
                axis=1,
            ).astype(BF16)
            summed = jnp.dot(member, lines, preferred_element_type=F32)
            for c in range(CHIPS):
                both = summed[c * REQ : (c + 1) * REQ]
                pay[home_core, c, tile] = jnp.concatenate(
                    [both[:, :DIM], both[:, DIM:]], axis=0
                ).astype(BF16)

    sum_slots(1 - core)
    to_sibling = remote(pay.at[1 - core], epay, e_s.at[0], e_r.at[0], sibling, tp)
    aux_to_sibling = remote(aux.at[1 - core], eaux, e_s.at[1], e_r.at[1], sibling, tp)
    aux_to_sibling.start()
    to_sibling.start()
    sum_slots(core)
    aux_to_sibling.wait()
    to_sibling.wait()

    def join(k, into, aux_into):
        home = chip ^ k
        a, b = aux[core, home], eaux[home]
        high = jnp.maximum(a, b)
        wa, wb = jnp.exp(a - high), jnp.exp(b - high)
        total = pltpu.roll(wa, LINES, 1) * a + pltpu.roll(wb, LINES, 1) * b
        aux_into[k] = jnp.where(lane < LINES, high, total)
        for tile in range(TILES):
            into[k, tile] = (
                spread(wa, tile) * pay[core, home, tile].astype(F32)
                + spread(wb, tile) * epay[home, tile].astype(F32)
            ).astype(BF16)

    def reduce_pay(k):
        return remote(cpay.at[k], rpay.at[k], rs_s.at[k], rs_r.at[k], me ^ (2 * k), tp)

    def reduce_aux(k):
        return remote(caux.at[k], raux.at[k], ra_s.at[k], ra_r.at[k], me ^ (2 * k), tp)

    @pl.loop(0, CHIPS - 1)
    def _(i):
        k = CHIPS - 1 - i
        join(k, cpay, caux)
        reduce_aux(k).start()
        reduce_pay(k).start()

    join(0, rpay, raux)

    @pl.loop(1, CHIPS)
    def _(k):
        reduce_aux(k).wait_recv()

    def high_step(k, x):
        return jnp.maximum(x, raux[k])

    peak = lax.fori_loop(0, CHIPS, high_step, dmax[...])
    draft_weight = jnp.exp(dmax[...] - peak)

    def total_step(k, x):
        weight = jnp.exp(raux[k] - peak)
        ew[k] = weight
        return x + weight * pltpu.roll(raux[k], DIM - LINES, 1)

    total = lax.fori_loop(0, CHIPS, total_step, draft_weight * dsum[...])
    scale = 1.0 / total
    draft_weight = draft_weight * scale
    for tile in range(TILES):
        first, second = tile_lines(tile)
        acc[tile] = spread(draft_weight, tile) * jnp.concatenate(
            [dval[pl.ds(first, REQ, stride=LINES), :], dval[pl.ds(second, REQ, stride=LINES), :]],
            axis=0,
        )

    def add_source(k):
        weight = ew[k] * scale
        for tile in range(TILES):
            acc[tile] += spread(weight, tile) * rpay[k, tile].astype(F32)

    add_source(0)

    @pl.loop(1, CHIPS)
    def _(k):
        reduce_pay(k).wait_recv()
        add_source(k)

    @pl.loop(1 + EARLY, INSTS)
    def _(k):
        migrate(k).start()

    for tile in range(TILES):
        t, g = tile // HEADS, tile % HEADS
        att[t * 16 : (t + 1) * 16, g * DIM : (g + 1) * DIM] = acc[tile].astype(BF16)

    w_load.wait()

    def project(k):
        columns = pl.ds(pl.multiple_of(lax.rem(tp + k, TPS) * COLS, COLS), COLS)
        return jnp.dot(att[...], w[:, columns], preferred_element_type=F32)

    def send_columns(k):
        return remote(
            zsend.at[k], zrecv.at[k], z_s.at[k], z_r.at[k], me, lax.rem(tp + k, TPS)
        )

    @pl.loop(1, TPS)
    def _(k):
        zsend[k] = project(k).astype(BF16)
        send_columns(k).start()

    zout[...] = project(0)

    @pl.loop(1, TPS)
    def _(k):
        send_columns(k).wait_recv()
        zout[...] += zrecv[k].astype(F32)

    for t in range(DRAFTS):
        for c in range(COLS // DIM):
            zsend_rows = zout[t * REQ : (t + 1) * REQ, c * DIM : (c + 1) * DIM]
            acc_rows = pl.ds(t, REQ, stride=DRAFTS)
            dval[pl.ds(c * 32 + t, REQ, stride=DRAFTS), :] = zsend_rows
    for c in range(COLS // DIM):
        out[:, c * DIM : (c + 1) * DIM] = dval[c * 32 : (c + 1) * 32, :].astype(BF16)

    @pl.loop(1, CHIPS)
    def _(k):
        gather_in(k).wait_send()
        reduce_aux(k).wait_send()
        reduce_pay(k).wait_send()

    @pl.loop(0, CHIPS)
    def _(k):
        gather_on(k).wait_send()

    @pl.loop(1, TPS)
    def _(k):
        send_columns(k).wait_send()

    @pl.loop(1, INSTS)
    def _(k):
        migrate(k).wait()

    own.wait()


def shards(queries, new_kv, kv_cache, block_owner, block_fill, move_slot, move_target, out_weight):
    vmem = pl.BlockSpec(memory_space=pltpu.VMEM)
    smem = pl.BlockSpec(memory_space=pltpu.SMEM)
    anywhere = pl.BlockSpec(memory_space=pl.ANY)
    dma = pltpu.SemaphoreType.DMA
    out, moved = pl.pallas_call(
        kernel,
        out_shape=(
            jax.ShapeDtypeStruct((DRAFTS * REQ, COLS), BF16),
            jax.ShapeDtypeStruct((SLOTS, 2, ROWS, DIM), BF16),
        ),
        in_specs=[vmem, vmem, anywhere, smem, smem, vmem, vmem, vmem, anywhere],
        out_specs=(vmem, anywhere),
        scratch_shapes=[
            pltpu.VMEM((SLOTS + 1, 2, ROWS, DIM), BF16),
            pltpu.VMEM((HEADS * DIM, TPS * COLS), BF16),
            pltpu.VMEM((8, DIM), I32),
            pltpu.SMEM((8, DIM), I32),
            pltpu.VMEM((SLOTS, 2, ROWS, DIM), BF16),
            pltpu.VMEM((REQS, LINES, DIM), BF16),
            pltpu.VMEM((REQ, 2, 8, DIM), F32),
            pltpu.VMEM((REQ * LINES, DIM), F32),
            pltpu.VMEM((REQ, DIM), F32),
            pltpu.VMEM((REQ, DIM), F32),
            pltpu.VMEM((GROUPS, ROWS, DIM), F32),
            pltpu.VMEM((GROUPS, DIM), F32),
            pltpu.VMEM((GROUPS, DIM), F32),
            pltpu.VMEM((REQS, DIM), F32),
            pltpu.VMEM((REQS, DIM), F32),
            pltpu.VMEM((SLOTS * LINES, DIM), F32),
            pltpu.VMEM((2, CHIPS, TILES, 16, DIM), BF16),
            pltpu.VMEM((2, CHIPS, REQ, DIM), F32),
            pltpu.VMEM((CHIPS, TILES, 16, DIM), BF16),
            pltpu.VMEM((CHIPS, REQ, DIM), F32),
            pltpu.VMEM((CHIPS, TILES, 16, DIM), BF16),
            pltpu.VMEM((CHIPS, REQ, DIM), F32),
            pltpu.VMEM((CHIPS, TILES, 16, DIM), BF16),
            pltpu.VMEM((CHIPS, REQ, DIM), F32),
            pltpu.VMEM((CHIPS, REQ, DIM), F32),
            pltpu.VMEM((TILES, 16, DIM), F32),
            pltpu.VMEM((DRAFTS * REQ, HEADS * DIM), BF16),
            pltpu.VMEM((TPS, DRAFTS * REQ, COLS), BF16),
            pltpu.VMEM((TPS, DRAFTS * REQ, COLS), BF16),
            pltpu.VMEM((DRAFTS * REQ, COLS), F32),
            dma((3,)), dma,
            dma((CHIPS,)), dma((CHIPS,)), dma((CHIPS,)), dma((CHIPS,)),
            dma((INSTS,)), dma((INSTS,)), dma((2,)), dma((2,)),
            dma((CHIPS,)), dma((CHIPS,)), dma((CHIPS,)), dma((CHIPS,)),
            dma((TPS,)), dma((TPS,)),
        ],
        compiler_params=pltpu.CompilerParams(
            collective_id=0, has_side_effects=True, vmem_limit_bytes=48 << 20
        ),
        name="decode",
    )(
        queries.reshape(REQ, LINES, DIM),
        new_kv.reshape(REQ, 2, DRAFTS, DIM),
        kv_cache.reshape(SLOTS, 2, ROWS, DIM),
        block_owner,
        block_fill,
        move_slot.reshape(MOVES, 1),
        move_target,
        move_target.reshape(1, MOVES),
        out_weight,
    )
    return out, moved.reshape(kv_cache.shape)


def solution(mesh):
    placed = (
        P("inst", None, "tp", None),
        P("inst", None, None, "tp", None),
        P("inst", None, "tp", None, None),
        P("inst"),
        P("inst"),
        P("inst"),
        P("inst", None),
        P("tp", None),
    )
    return jax.shard_map(
        shards,
        mesh=mesh,
        in_specs=placed,
        out_specs=(P("inst", "tp"), P("inst", None, "tp", None, None)),
        check_vma=False,
    )
```

time: 241 us -> 107 us (0.44)
  the two profiles are of different devices: /device:TPU:2 before, /device:TPU:1 now
where the time goes in v1:
time: 107 us; the launch traced here: 106 us
  Pallas kernels  97.2 us (91%)
  local copies, waits for them, and re-layouts  8.51 us (8%)
    pallas_call x1, Pallas kernels, shards(): pl.pallas_call(kernel, out_shape=(jax.ShapeDtypeStruct((DRAFTS * REQ, COL...  97.2 us
    unnamed x15, local copies, waits for them, and re-layouts  7.78 us

profile of v1, /device:TPU:1, one launch (start us, length us, event | category | flops | bytes accessed | tf_op | source)
XLA Modules:
  0.0 106.4 jit_solution(16697251510297523914)
XLA Ops:
  0.6 0.7 copy.10.slot_col
  1.4 0.7 copy.11.target_col
  2.1 0.0 copy-start
  2.1 1.6 %copy-done = bf16[64,2,1,64,128]{4,3,2,1,0:T(8,128)(2,1)S(1)} copy-done((bf16[64,2,1,64,128]{4,3,2,1,0:T(8,128)(2,1)S(1)}, bf16[64,2,1,64,128]{4,3,2,1,0:T(8,128)(2,1)}, u32[]{:S(2)}) %copy-start) | copy-done | bytes 2097176
  3.7 0.0 copy-start.1
  3.7 0.8 copy-done.1
  4.5 0.0 copy-start.2
  4.5 0.7 copy-done.2
  5.2 0.0 copy-start.3
  5.2 0.7 copy-done.3
  5.9 0.0 copy-start.4
  5.9 0.7 copy-done.4
  6.6 0.0 copy-start.5
  6.6 0.7 copy-done.5
  7.2 97.2 %decode.1 = (bf16[32,512]{1,0:T(8,128)(2,1)S(1)}, bf16[64,2,64,128]{3,2,1,0:T(8,128)(2,1)S(1)}) custom-call(bf16[8,32,128]{2,1,0:T(8,128)(2,1)S(1)} %bitcast.10, bf16[8,2,4,128]{3,2,1,0:T(4,128)(2,1)S(1)} %bitcast.11, bf16[64,2,64,128]{3,2,1,0:T(8,128)(2,1)S(1)} %bitcast.8, s32[64]{0:T(128)S(1)} %copy-done.4, s32[64]{0:T(128)S(1)} %copy-done.5, ...), custom_call_target="tpu_custom_call" | custom-call | tf_op jit(solution)/shard_map/decode/pallas_call | solution.py:416
  104.5 0.6 copy.15
  105.1 1.3 %copy.16 = bf16[64,2,1,64,128]{4,3,2,1,0:T(8,128)(2,1)} copy(bf16[64,2,1,64,128]{4,3,2,1,0:T(8,128)(2,1)S(1)} %bitcast.9) | data formatting | bytes 4194304
Async XLA Ops:
  2.1 1.6 %copy-start = (bf16[64,2,1,64,128]{4,3,2,1,0:T(8,128)(2,1)S(1)}, bf16[64,2,1,64,128]{4,3,2,1,0:T(8,128)(2,1)}, u32[]{:S(2)}) copy-start(bf16[64,2,1,64,128]{4,3,2,1,0:T(8,128)(2,1)} %param.10) | copy-start | bytes 6291460
  3.7 0.8 copy-start.1
  4.5 0.7 copy-start.2
  5.2 0.7 copy-start.3
  5.9 0.7 copy-start.4
  6.6 0.7 copy-start.5

commit v2 on v1

v2 whole, which is shorter than its diff:
```python
import functools

import jax
import jax.numpy as jnp
from jax import lax
from jax.experimental import pallas as pl
from jax.experimental.pallas import tpu as pltpu
from jax.sharding import PartitionSpec as P

MESH = pl.DeviceIdType.MESH
MASKED = -1e30
CAPACITY = 2
F32, BF16, I32 = jnp.float32, jnp.bfloat16, jnp.int32

INSTS = 32
CHIPS = 16
TPS = 8
SLOTS = 64
ROWS = 64
DIM = 128
HEADS = 8
DRAFTS = 4
LINES = DRAFTS * HEADS
REQ = 8
REQS = INSTS * REQ
GROUPS = SLOTS // 4
TILES = LINES // 2
COLS = 512
MOVES = 24
EARLY = 12
WIDE = 2


def nt_dot(a, b):
    return lax.dot_general(a, b, (((1,), (1,)), ((), ())), preferred_element_type=F32)


def tile_lines(tile):
    t, g = 2 * (tile // HEADS), tile % HEADS
    return t * HEADS + g, (t + 1) * HEADS + g


def spread(weights, tile):
    first, second = tile_lines(tile)
    return jnp.concatenate(
        [
            jnp.broadcast_to(weights[:, first : first + 1], (REQ, DIM)),
            jnp.broadcast_to(weights[:, second : second + 1], (REQ, DIM)),
        ],
        axis=0,
    )


def kernel(
    q_hbm, nkv_hbm, kv_hbm, owner_hbm, fill_hbm, slot_hbm, target_hbm, w_hbm,
    out, moved,
    q, nkv, kv, w, owner, fill, slot, target, pick, pick_s, msend, qall, dkv, dval, dmax, dsum,
    score, smax, ssum, reqmax, reqsum, val, pay, aux, epay, eaux, cpay, caux,
    rpay, raux, spay, saux, fpay, faux, acc, att, zsend, zrecv, zout,
    load_sem, own_sem, ag_s, ag_r, sib_s, sib_r, mig_s, mig_r, e_s, e_r,
    p_s, p_r, a_s, a_r, fp_s, fp_r, fa_s, fa_r, z_s, z_r,
):
    me, tp = lax.axis_index("inst"), lax.axis_index("tp")
    core = lax.rem(me, 2)
    chip = me // 2
    sibling = me ^ 1

    def remote(src, dst, send, recv, inst, z):
        return pltpu.make_async_remote_copy(
            src_ref=src, dst_ref=dst, send_sem=send, recv_sem=recv,
            device_id=(inst, z), device_id_type=MESH,
        )

    barrier = pltpu.get_barrier_semaphore()

    @pl.loop(1, INSTS)
    def _(k):
        pl.semaphore_signal(barrier, inc=1, device_id=(me ^ k, tp), device_id_type=MESH)

    @pl.loop(1, TPS)
    def _(k):
        pl.semaphore_signal(barrier, inc=1, device_id=(me, tp ^ k), device_id_type=MESH)

    loads = [
        pltpu.make_async_copy(src, dst, load_sem.at[i])
        for i, (src, dst) in enumerate(
            [
                (q_hbm, q),
                (slot_hbm, slot),
                (target_hbm, target),
                (nkv_hbm, nkv),
                (owner_hbm, owner),
                (fill_hbm, fill),
                (kv_hbm, kv.at[pl.ds(0, SLOTS)]),
                (w_hbm, w),
                (pick, pick_s),
            ]
        )
    ]
    q_load, slot_load, target_load, nkv_load, owner_load, fill_load, kv_load, w_load, pick_load = loads
    for load in loads[:-1]:
        load.start()

    lane = lax.broadcasted_iota(I32, (1, DIM), 1)
    lane_group = lane // LINES

    def by_group(parts):
        return jnp.where(
            lane_group == 0,
            parts[0],
            jnp.where(lane_group == 1, parts[1], jnp.where(lane_group == 2, parts[2], parts[3])),
        )

    kv[SLOTS] = jnp.zeros((2, ROWS, DIM), BF16)
    dkv[...] = jnp.zeros(dkv.shape, F32)
    slot_load.wait()
    target_load.wait()
    pick_first = jnp.full((1, DIM), SLOTS, I32)
    pick_second = pick_first
    for j in range(MOVES):
        hit = lane == target[j]
        again = hit & (pick_first != SLOTS)
        pick_second = jnp.where(again, slot[j], pick_second)
        pick_first = jnp.where(hit & (pick_first == SLOTS), slot[j], pick_first)
    pick[...] = jnp.concatenate([pick_first, pick_second] * 4, axis=0)
    pick_load.start()

    def drafts():
        dkv[:, :, 0:DRAFTS, :] = nkv[...].astype(F32)
        for half in range(REQ // 4):
            queries = q[4 * half : 4 * half + 4].reshape(4 * LINES, DIM)
            keys = dkv[4 * half : 4 * half + 4, 0].reshape(4 * 8, DIM).astype(BF16)
            full = nt_dot(keys, queries)
            scores = by_group([full[8 * i : 8 * i + 8] for i in range(4)]) * (DIM**-0.5)
            u = lax.broadcasted_iota(I32, (8, DIM), 0)
            t = lax.rem(lax.broadcasted_iota(I32, (8, DIM), 1), LINES) // HEADS
            causal = u <= t
            high = jnp.max(jnp.where(causal, scores, MASKED), axis=0, keepdims=True)
            probs = jnp.where(causal, jnp.exp(scores - high), 0.0)
            total = jnp.sum(probs, axis=0, keepdims=True)
            turned = jnp.transpose(probs).astype(BF16)
            for i in range(4):
                r = 4 * half + i
                dmax[r : r + 1, :] = high if i == 0 else pltpu.roll(high, DIM - i * LINES, 1)
                dsum[r : r + 1, :] = total if i == 0 else pltpu.roll(total, DIM - i * LINES, 1)
                dval[r * LINES : (r + 1) * LINES, :] = jnp.dot(
                    turned[i * LINES : (i + 1) * LINES],
                    dkv[r, 1].astype(BF16),
                    preferred_element_type=F32,
                )

    q_load.wait()
    qall[pl.ds(me * 2, 2)] = q[...].reshape(2, REQ // 2, LINES, DIM)

    def chunk(kx, ky, h):
        return qall.at[(me ^ (kx * 8 + ky * 2)) * 2 + h]

    def gather(kx, ky, h):
        first, on = ((kx * 8, ky * 2), (ky * 2, kx * 8))[h]
        if on == 0:
            src, to = chunk(0, 0, h), me ^ first
        else:
            src, to = (chunk(kx, 0, h), chunk(0, ky, h))[h], me ^ on
        at = h * CHIPS + kx * 4 + ky
        return remote(src, src, ag_s.at[at], ag_r.at[at], to, tp)

    def arrived(kx, ky, h):
        at = h * CHIPS + kx * 4 + ky
        ref = chunk(kx, ky, h)
        return remote(ref, ref, ag_s.at[at], ag_r.at[at], sibling, tp)

    def gather_on(kx, ky, h):
        at = h * CHIPS + kx * 4 + ky
        ref = chunk(kx, ky, h)
        return remote(ref, ref, sib_s.at[at], sib_r.at[at], sibling, tp)

    order = (1, 3, 2)
    pl.semaphore_wait(barrier, INSTS - 1 + TPS - 1)
    for k in (2, 1, 3):
        gather(k, 0, 0).start()
        gather(0, k, 1).start()
    for k in (2, 1, 3):
        gather(0, k, 0).start()
        gather(k, 0, 1).start()
    gather_on(0, 0, 0).start()
    gather_on(0, 0, 1).start()
    nkv_load.wait()
    drafts()
    for a in order:
        arrived(a, 0, 0).wait_recv()
        for b in (2, 1, 3):
            gather(a, b, 0).start()
        arrived(0, a, 1).wait_recv()
        for b in (2, 1, 3):
            gather(b, a, 1).start()
        gather_on(a, 0, 0).start()
        gather_on(0, a, 1).start()

    kv_load.wait()
    pick_load.wait()

    @pl.loop(0, INSTS)
    def _(d):
        for i in range(CAPACITY):
            msend[CAPACITY * d + i] = kv[pick_s[i, d]]

    for a in (0,) + order:
        for b in order:
            arrived(a, b, 0).wait_recv()
            gather_on(a, b, 0).start()
            arrived(b, a, 1).wait_recv()
            gather_on(b, a, 1).start()

    own = pltpu.make_async_copy(
        msend.at[pl.ds(CAPACITY * me, CAPACITY)],
        moved.at[pl.ds(CAPACITY * me, CAPACITY)],
        own_sem,
    )
    own.start()

    def migrate(i):
        k = lax.rem(i * 11, INSTS)
        return remote(
            msend.at[pl.ds(CAPACITY * (me ^ k), CAPACITY)],
            moved.at[pl.ds(CAPACITY * me, CAPACITY)],
            mig_s.at[k], mig_r.at[k], me ^ k, tp,
        )

    @pl.loop(1, 1 + EARLY)
    def _(i):
        migrate(i).start()

    owner_load.wait()
    fill_load.wait()
    for a in range(4):
        for b in range(4):
            for h in range(2):
                gather_on(a, b, h).wait_recv()

    row_of = lax.broadcasted_iota(I32, (ROWS, DIM), 0)

    def usable(g):
        return row_of < by_group([fill[4 * g + i] for i in range(4)])

    def score_group(g):
        queries = jnp.concatenate(
            [qall[owner[4 * g + i] // 4, lax.rem(owner[4 * g + i], 4)] for i in range(4)], axis=0
        )
        keys = kv[pl.ds(4 * g, 4), 0].reshape(4 * ROWS, DIM)
        full = nt_dot(keys, queries)
        scores = by_group([full[ROWS * i : ROWS * (i + 1)] for i in range(4)]) * (DIM**-0.5)
        scores = jnp.where(usable(g), scores, MASKED)
        return scores, jnp.max(scores, axis=0, keepdims=True)

    row = lax.broadcasted_iota(I32, (REQS, DIM), 0)
    request = (row % (REQS // 2)) // REQ * (2 * REQ) + row // (REQS // 2) * REQ + row % REQ

    def owners(g):
        return by_group([owner[4 * g + i] for i in range(4)])

    def all_groups(x, f):
        x = f(x, pltpu.roll(x, 2 * LINES, 1))
        return f(x, pltpu.roll(x, LINES, 1))

    def weigh_group(g, scores):
        highs = []
        for i in range(4):
            o = owner[4 * g + i]
            at = lax.rem(o // REQ, 2) * (REQS // 2) + o // (2 * REQ) * REQ + lax.rem(o, REQ)
            highs.append(reqmax[pl.ds(at, 1), :])
        probs = jnp.where(usable(g), jnp.exp(scores - by_group(highs)), 0.0)
        turned = jnp.transpose(probs).astype(BF16)
        return jnp.sum(probs, axis=0, keepdims=True), [
            jnp.dot(
                turned[i * LINES : (i + 1) * LINES],
                kv[4 * g + i, 1],
                preferred_element_type=F32,
            )
            for i in range(4)
        ]

    @pl.loop(0, GROUPS // WIDE)
    def _(s):
        for g in [s * WIDE + i for i in range(WIDE)]:
            score[g], smax[pl.ds(g, 1), :] = score_group(g)

    reqmax[...] = jnp.full(reqmax.shape, MASKED, F32)

    @pl.loop(0, GROUPS // 4)
    def _(s):
        high = reqmax[...]
        for g in [s * 4 + i for i in range(4)]:
            high = jnp.where(
                request == owners(g), jnp.maximum(high, smax[pl.ds(g, 1), :]), high
            )
        reqmax[...] = high

    reqmax[...] = all_groups(reqmax[...], jnp.maximum)

    @pl.loop(0, GROUPS // WIDE)
    def _(s):
        groups = [s * WIDE + i for i in range(WIDE)]
        done = [weigh_group(g, score[g]) for g in groups]
        for g, (total, values) in zip(groups, done):
            ssum[pl.ds(g, 1), :] = total
            for i in range(4):
                val[pl.ds((4 * g + i) * LINES, LINES), :] = values[i]

    reqsum[...] = jnp.zeros(reqsum.shape, F32)

    @pl.loop(0, GROUPS // 4)
    def _(s):
        total = reqsum[...]
        for g in [s * 4 + i for i in range(4)]:
            total += jnp.where(request == owners(g), ssum[pl.ds(g, 1), :], 0.0)
        reqsum[...] = total

    reqsum[...] = all_groups(reqsum[...], jnp.add)
    aux[...] = jnp.where(lane < LINES, reqmax[...], reqsum[...]).reshape(aux.shape)

    owner_lane = lax.broadcasted_iota(I32, (1, SLOTS), 1)

    def owner_step(b, x):
        return jnp.where(owner_lane == b, owner[b], x)

    half_row = lax.broadcasted_iota(I32, (REQS // 2, SLOTS), 0)

    def sum_slots(home_core, half, owner_row):
        ids = half_row // REQ * (2 * REQ) + home_core * REQ + half_row % REQ
        member = (ids == owner_row).astype(F32).astype(BF16)

        @pl.loop(0, HEADS // 2)
        def _(s):
            done = []
            for g in [s * 2 + i for i in range(2)]:
                first = 2 * HEADS * half + g
                lines = jnp.concatenate(
                    [
                        val[pl.ds(first, SLOTS, stride=LINES), :],
                        val[pl.ds(first + HEADS, SLOTS, stride=LINES), :],
                    ],
                    axis=1,
                ).astype(BF16)
                done.append((g, jnp.dot(member, lines, preferred_element_type=F32)))
            for g, summed in done:
                for c in range(CHIPS):
                    both = summed[c * REQ : (c + 1) * REQ]
                    pay[home_core, half, c, g] = jnp.concatenate(
                        [both[:, :DIM], both[:, DIM:]], axis=0
                    ).astype(BF16)

    def join_cores(half):
        return remote(pay.at[1 - core, half], epay.at[half], e_s.at[half], e_r.at[half], sibling, tp)

    aux_join = remote(aux.at[1 - core], eaux, e_s.at[2], e_r.at[2], sibling, tp)

    def join(half, k, into, aux_into):
        @pl.loop(0, 4)
        def _(m):
            home = chip ^ (k * 4 + m if half == 0 else m * 4 + k)
            a, b = aux[core, home], eaux[home]
            high = jnp.maximum(a, b)
            wa, wb = jnp.exp(a - high), jnp.exp(b - high)
            total = pltpu.roll(wa, LINES, 1) * a + pltpu.roll(wb, LINES, 1) * b
            aux_into[half, k, m] = jnp.where(lane < LINES, high, total)
            for g in range(HEADS):
                tile = half * HEADS + g
                into[half, k, m, g] = (
                    spread(wa, tile) * pay[core, half, home, g].astype(F32)
                    + spread(wb, tile) * epay[half, home, g].astype(F32)
                ).astype(BF16)

    def step_of(half, k):
        return me ^ (k * 8 if half == 0 else k * 2)

    def first_pay(half, k):
        at = half * 4 + k
        return remote(
            cpay.at[half, k], rpay.at[half, k], p_s.at[at], p_r.at[at], step_of(half, k), tp
        )

    def first_aux(half, k):
        at = half * 4 + k
        return remote(
            caux.at[half, k], raux.at[half, k], a_s.at[at], a_r.at[at], step_of(half, k), tp
        )

    def second_pay(half, m):
        at = half * 4 + m
        return remote(
            spay.at[half, m], fpay.at[half, m], fp_s.at[at], fp_r.at[at], step_of(1 - half, m), tp
        )

    def second_aux(half, m):
        at = half * 4 + m
        return remote(
            saux.at[half, m], faux.at[half, m], fa_s.at[at], fa_r.at[at], step_of(1 - half, m), tp
        )

    def merge(half, m, into, aux_into):
        parts = [raux[half, k, m] for k in range(4)]
        high = functools.reduce(jnp.maximum, parts)
        weights = [jnp.exp(part - high) for part in parts]
        total = sum(pltpu.roll(wt, LINES, 1) * part for wt, part in zip(weights, parts))
        aux_into[half, m] = jnp.where(lane < LINES, high, total)
        for g in range(HEADS):
            tile = half * HEADS + g
            into[half, m, g] = sum(
                spread(weights[k], tile) * rpay[half, k, m, g].astype(F32) for k in range(4)
            ).astype(BF16)

    aux_join.start()
    owner_row = lax.fori_loop(0, SLOTS, owner_step, jnp.zeros((1, SLOTS), I32))
    for half in range(2):
        sum_slots(1 - core, half, owner_row)
        join_cores(half).start()
    for half in range(2):
        sum_slots(core, half, owner_row)
    aux_join.wait()
    join_cores(0).wait()
    join_cores(1).wait()

    for k in (2, 1, 3):
        for half in range(2):
            join(half, k, cpay, caux)
            first_aux(half, k).start()
            first_pay(half, k).start()
    for half in range(2):
        join(half, 0, rpay, raux)
    for k in (1, 3, 2):
        for half in range(2):
            first_aux(half, k).wait_recv()
            first_pay(half, k).wait_recv()
    for m in (2, 1, 3):
        for half in range(2):
            merge(half, m, spay, saux)
            second_aux(half, m).start()
            second_pay(half, m).start()
    for half in range(2):
        merge(half, 0, fpay, faux)
    for half in range(2):
        for m in (1, 3, 2):
            second_aux(half, m).wait_recv()

    parts = [
        jnp.where(lane % LINES < LINES // 2, faux[0, m], faux[1, m]) for m in range(4)
    ]
    peak = functools.reduce(jnp.maximum, parts, dmax[...])
    weights = [jnp.exp(part - peak) for part in parts]
    draft_weight = jnp.exp(dmax[...] - peak)
    total = draft_weight * dsum[...] + sum(
        wt * pltpu.roll(part, DIM - LINES, 1) for wt, part in zip(weights, parts)
    )
    scale = 1.0 / total
    weights = [wt * scale for wt in weights]
    draft_weight = draft_weight * scale
    for tile in range(TILES):
        first, second = tile_lines(tile)
        acc[tile] = spread(draft_weight, tile) * jnp.concatenate(
            [
                dval[pl.ds(first, REQ, stride=LINES), :],
                dval[pl.ds(second, REQ, stride=LINES), :],
            ],
            axis=0,
        )
    for half in range(2):
        for m in (1, 3, 2):
            second_pay(half, m).wait_recv()
    for tile in range(TILES):
        half, g = tile // HEADS, tile % HEADS
        line = acc[tile] + sum(
            spread(weights[m], tile) * fpay[half, m, g].astype(F32) for m in range(4)
        )
        att[half * 16 : (half + 1) * 16, g * DIM : (g + 1) * DIM] = line.astype(BF16)

    @pl.loop(1 + EARLY, INSTS)
    def _(i):
        migrate(i).start()

    w_load.wait()

    def project(k):
        columns = pl.ds(pl.multiple_of(lax.rem(tp + k, TPS) * COLS, COLS), COLS)
        return jnp.dot(att[...], w[:, columns], preferred_element_type=F32)

    def send_columns(k):
        return remote(
            zsend.at[k], zrecv.at[k], z_s.at[k], z_r.at[k], me, lax.rem(tp + k, TPS)
        )

    for k in (4, 3, 5, 2, 6, 1, 7):
        zsend[k] = project(k).astype(BF16)
        send_columns(k).start()

    zout[...] = project(0)

    for k in (1, 7, 2, 6, 3, 5, 4):
        send_columns(k).wait_recv()
        zout[...] += zrecv[k].astype(F32)

    for t in range(DRAFTS):
        for c in range(COLS // DIM):
            dval[pl.ds(c * 32 + t, REQ, stride=DRAFTS), :] = zout[
                t * REQ : (t + 1) * REQ, c * DIM : (c + 1) * DIM
            ]
    for c in range(COLS // DIM):
        out[:, c * DIM : (c + 1) * DIM] = dval[c * 32 : (c + 1) * 32, :].astype(BF16)

    for a in range(4):
        for b in range(4):
            for h in range(2):
                if (a, b) != (0, 0):
                    gather(a, b, h).wait_send()
                gather_on(a, b, h).wait_send()
    own.wait()
    for half in range(2):
        for k in range(1, 4):
            first_aux(half, k).wait_send()
            first_pay(half, k).wait_send()
            second_aux(half, k).wait_send()
            second_pay(half, k).wait_send()
    for k in range(1, TPS):
        send_columns(k).wait_send()
    @pl.loop(1, INSTS)
    def _(i):
        migrate(i).wait()


def shards(queries, new_kv, kv_cache, block_owner, block_fill, move_slot, move_target, out_weight):
    vmem = pl.BlockSpec(memory_space=pltpu.VMEM)
    anywhere = pl.BlockSpec(memory_space=pl.ANY)
    dma = pltpu.SemaphoreType.DMA
    out, moved = pl.pallas_call(
        kernel,
        out_shape=(
            jax.ShapeDtypeStruct((DRAFTS * REQ, COLS), BF16),
            jax.ShapeDtypeStruct((SLOTS, 2, ROWS, DIM), BF16),
        ),
        in_specs=[anywhere] * 8,
        out_specs=(vmem, anywhere),
        scratch_shapes=[
            pltpu.VMEM((REQ, LINES, DIM), BF16),
            pltpu.VMEM((REQ, 2, DRAFTS, DIM), BF16),
            pltpu.VMEM((SLOTS + 1, 2, ROWS, DIM), BF16),
            pltpu.VMEM((HEADS * DIM, TPS * COLS), BF16),
            pltpu.SMEM((SLOTS,), I32),
            pltpu.SMEM((SLOTS,), I32),
            pltpu.SMEM((MOVES,), I32),
            pltpu.SMEM((MOVES,), I32),
            pltpu.VMEM((8, DIM), I32),
            pltpu.SMEM((8, DIM), I32),
            pltpu.VMEM((SLOTS, 2, ROWS, DIM), BF16),
            pltpu.VMEM((INSTS * 2, REQ // 2, LINES, DIM), BF16),
            pltpu.VMEM((REQ, 2, 8, DIM), F32),
            pltpu.VMEM((REQ * LINES, DIM), F32),
            pltpu.VMEM((REQ, DIM), F32),
            pltpu.VMEM((REQ, DIM), F32),
            pltpu.VMEM((GROUPS, ROWS, DIM), F32),
            pltpu.VMEM((GROUPS, DIM), F32),
            pltpu.VMEM((GROUPS, DIM), F32),
            pltpu.VMEM((REQS, DIM), F32),
            pltpu.VMEM((REQS, DIM), F32),
            pltpu.VMEM((SLOTS * LINES, DIM), F32),
            pltpu.VMEM((2, 2, CHIPS, HEADS, 16, DIM), BF16),
            pltpu.VMEM((2, CHIPS, REQ, DIM), F32),
            pltpu.VMEM((2, CHIPS, HEADS, 16, DIM), BF16),
            pltpu.VMEM((CHIPS, REQ, DIM), F32),
            pltpu.VMEM((2, 4, 4, HEADS, 16, DIM), BF16),
            pltpu.VMEM((2, 4, 4, REQ, DIM), F32),
            pltpu.VMEM((2, 4, 4, HEADS, 16, DIM), BF16),
            pltpu.VMEM((2, 4, 4, REQ, DIM), F32),
            pltpu.VMEM((2, 4, HEADS, 16, DIM), BF16),
            pltpu.VMEM((2, 4, REQ, DIM), F32),
            pltpu.VMEM((2, 4, HEADS, 16, DIM), BF16),
            pltpu.VMEM((2, 4, REQ, DIM), F32),
            pltpu.VMEM((TILES, 16, DIM), F32),
            pltpu.VMEM((DRAFTS * REQ, HEADS * DIM), BF16),
            pltpu.VMEM((TPS, DRAFTS * REQ, COLS), BF16),
            pltpu.VMEM((TPS, DRAFTS * REQ, COLS), BF16),
            pltpu.VMEM((DRAFTS * REQ, COLS), F32),
            dma((9,)), dma,
            dma((2 * CHIPS,)), dma((2 * CHIPS,)), dma((2 * CHIPS,)), dma((2 * CHIPS,)),
            dma((INSTS,)), dma((INSTS,)), dma((3,)), dma((3,)),
            dma((8,)), dma((8,)), dma((8,)), dma((8,)),
            dma((8,)), dma((8,)), dma((8,)), dma((8,)),
            dma((TPS,)), dma((TPS,)),
        ],
        compiler_params=pltpu.CompilerParams(
            collective_id=0, has_side_effects=True, vmem_limit_bytes=63 << 20
        ),
        name="decode",
    )(
        queries.reshape(REQ, LINES, DIM),
        new_kv.reshape(REQ, 2, DRAFTS, DIM),
        kv_cache.reshape(SLOTS, 2, ROWS, DIM),
        block_owner,
        block_fill,
        move_slot,
        move_target.reshape(MOVES),
        out_weight,
    )
    return out, moved.reshape(kv_cache.shape)


def solution(mesh):
    placed = (
        P("inst", None, "tp", None),
        P("inst", None, None, "tp", None),
        P("inst", None, "tp", None, None),
        P("inst"),
        P("inst"),
        P("inst"),
        P("inst", None),
        P("tp", None),
    )
    return jax.shard_map(
        shards,
        mesh=mesh,
        in_specs=placed,
        out_specs=(P("inst", "tp"), P("inst", None, "tp", None, None)),
        check_vma=False,
    )
```

time: 107 us -> 75.6 us (0.71)
  Pallas kernels: 97.2 us -> 70.2 us
  local copies, waits for them, and re-layouts: 8.51 us -> 4.6 us
    pallas_call x1, Pallas kernels: 97.2 us -> 70.2 us  [shards(): pl.pallas_call(kernel, out_shape=(jax.ShapeDtypeStruct((DRAFTS * REQ, COL...]
    unnamed x15 -> x2, local copies, waits for them, and re-layouts: 7.78 us -> 4.6 us
where the time goes in v2:
time: 75.6 us; the launch traced here: 75.4 us
  Pallas kernels  70.2 us (93%)
  local copies, waits for them, and re-layouts  4.6 us (6%)
    pallas_call x1, Pallas kernels, shards(): pl.pallas_call(kernel, out_shape=(jax.ShapeDtypeStruct((DRAFTS * REQ, COL...  70.2 us
    unnamed x2, local copies, waits for them, and re-layouts  4.6 us

profile of v2, /device:TPU:1, one launch (start us, length us, event | category | flops | bytes accessed | tf_op | source)
XLA Modules:
  0.0 75.4 jit_solution(8725269926612379443)
XLA Ops:
  0.6 70.2 %decode.1 = (bf16[32,512]{1,0:T(8,128)(2,1)}, bf16[64,2,64,128]{3,2,1,0:T(8,128)(2,1)}) custom-call(bf16[8,32,128]{2,1,0:T(8,128)(2,1)} %bitcast.9, bf16[8,2,4,128]{3,2,1,0:T(4,128)(2,1)} %bitcast.10, bf16[64,2,64,128]{3,2,1,0:T(8,128)(2,1)} %bitcast.8, s32[64]{0:T(128)} %owner_hbm.1, s32[64]{0:T(128)} %fill_hbm.1, s32[24]{0:T(128)} %slot_hbm.1, ...), custom_call_target="tpu_custom_call" | custom-call | tf_op jit(solution)/shard_map/decode/pallas_call | solution.py:533
  70.8 1.4 %copy.13 = bf16[32,512]{1,0:T(8,128)(2,1)} copy(bf16[32,512]{1,0:T(8,128)(2,1)} %get-tuple-element.10) | data formatting | bytes 65536
  72.2 3.2 %copy.14 = bf16[64,2,1,64,128]{4,3,2,1,0:T(8,128)(2,1)} copy(bf16[64,2,1,64,128]{4,3,2,1,0:T(8,128)(2,1)} %bitcast.7) | data formatting | bytes 4194304

commit v3 on v2

--- a/solution.py
+++ b/solution.py
@@ -27,8 +27,10 @@
 TILES = LINES // 2
 COLS = 512
 MOVES = 24
-EARLY = 12
-WIDE = 2
+BATCHES = (8, 10, 2, 0, 4)
+WIDE = 4
+PARTS = 8
+SUMS = 4
 
 
 def nt_dot(a, b):
@@ -55,10 +57,10 @@
     q_hbm, nkv_hbm, kv_hbm, owner_hbm, fill_hbm, slot_hbm, target_hbm, w_hbm,
     out, moved,
     q, nkv, kv, w, owner, fill, slot, target, pick, pick_s, msend, qall, dkv, dval, dmax, dsum,
-    score, smax, ssum, reqmax, reqsum, val, pay, aux, epay, eaux, cpay, caux,
-    rpay, raux, spay, saux, fpay, faux, acc, att, zsend, zrecv, zout,
+    score, smax, ssum, reqmax, reqsum, val, pay, aux, epay, eaux, cpay,
+    rpay, spay, fpay, acc, att, zsend, zrecv, zout,
     load_sem, own_sem, ag_s, ag_r, sib_s, sib_r, mig_s, mig_r, e_s, e_r,
-    p_s, p_r, a_s, a_r, fp_s, fp_r, fa_s, fa_r, z_s, z_r,
+    p_s, p_r, fp_s, fp_r, z_s, z_r,
 ):
     me, tp = lax.axis_index("inst"), lax.axis_index("tp")
     core = lax.rem(me, 2)
@@ -174,7 +176,31 @@
         ref = chunk(kx, ky, h)
         return remote(ref, ref, sib_s.at[at], sib_r.at[at], sibling, tp)
 
+    def migrate(i):
+        k = lax.rem(i * 11, INSTS)
+        return remote(
+            msend.at[pl.ds(CAPACITY * (me ^ k), CAPACITY)],
+            moved.at[pl.ds(CAPACITY * me, CAPACITY)],
+            mig_s.at[k], mig_r.at[k], me ^ k, tp,
+        )
+
+    bounds = [1 + sum(BATCHES[:i]) for i in range(len(BATCHES) + 1)] + [INSTS]
+
+    def migrate_batch(i):
+        pl.loop(bounds[i], bounds[i + 1])(lambda k: migrate(k).start())
+
     order = (1, 3, 2)
+    nkv_load.wait()
+    drafts()
+
+    kv_load.wait()
+    pick_load.wait()
+
+    @pl.loop(0, INSTS)
+    def _(d):
+        for i in range(CAPACITY):
+            msend[CAPACITY * d + i] = kv[pick_s[i, d]]
+
     pl.semaphore_wait(barrier, INSTS - 1 + TPS - 1)
     for k in (2, 1, 3):
         gather(k, 0, 0).start()
@@ -184,8 +210,6 @@
         gather(k, 0, 1).start()
     gather_on(0, 0, 0).start()
     gather_on(0, 0, 1).start()
-    nkv_load.wait()
-    drafts()
     for a in order:
         arrived(a, 0, 0).wait_recv()
         for b in (2, 1, 3):
@@ -196,13 +220,7 @@
         gather_on(a, 0, 0).start()
         gather_on(0, a, 1).start()
 
-    kv_load.wait()
-    pick_load.wait()
-
-    @pl.loop(0, INSTS)
-    def _(d):
-        for i in range(CAPACITY):
-            msend[CAPACITY * d + i] = kv[pick_s[i, d]]
+    migrate_batch(0)
 
     for a in (0,) + order:
         for b in order:
@@ -218,18 +236,7 @@
     )
     own.start()
 
-    def migrate(i):
-        k = lax.rem(i * 11, INSTS)
-        return remote(
-            msend.at[pl.ds(CAPACITY * (me ^ k), CAPACITY)],
-            moved.at[pl.ds(CAPACITY * me, CAPACITY)],
-            mig_s.at[k], mig_r.at[k], me ^ k, tp,
-        )
-
-    @pl.loop(1, 1 + EARLY)
-    def _(i):
-        migrate(i).start()
-
+    migrate_batch(1)
     owner_load.wait()
     fill_load.wait()
     for a in range(4):
@@ -306,18 +313,6 @@
             for i in range(4):
                 val[pl.ds((4 * g + i) * LINES, LINES), :] = values[i]
 
-    reqsum[...] = jnp.zeros(reqsum.shape, F32)
-
-    @pl.loop(0, GROUPS // 4)
-    def _(s):
-        total = reqsum[...]
-        for g in [s * 4 + i for i in range(4)]:
-            total += jnp.where(request == owners(g), ssum[pl.ds(g, 1), :], 0.0)
-        reqsum[...] = total
-
-    reqsum[...] = all_groups(reqsum[...], jnp.add)
-    aux[...] = jnp.where(lane < LINES, reqmax[...], reqsum[...]).reshape(aux.shape)
-
     owner_lane = lax.broadcasted_iota(I32, (1, SLOTS), 1)
 
     def owner_step(b, x):
@@ -329,10 +324,10 @@
         ids = half_row // REQ * (2 * REQ) + home_core * REQ + half_row % REQ
         member = (ids == owner_row).astype(F32).astype(BF16)
 
-        @pl.loop(0, HEADS // 2)
+        @pl.loop(0, HEADS // SUMS)
         def _(s):
             done = []
-            for g in [s * 2 + i for i in range(2)]:
+            for g in [s * SUMS + i for i in range(SUMS)]:
                 first = 2 * HEADS * half + g
                 lines = jnp.concatenate(
                     [
@@ -354,35 +349,39 @@
 
     aux_join = remote(aux.at[1 - core], eaux, e_s.at[2], e_r.at[2], sibling, tp)
 
-    def join(half, k, into, aux_into):
-        @pl.loop(0, 4)
-        def _(m):
-            home = chip ^ (k * 4 + m if half == 0 else m * 4 + k)
-            a, b = aux[core, home], eaux[home]
-            high = jnp.maximum(a, b)
-            wa, wb = jnp.exp(a - high), jnp.exp(b - high)
-            total = pltpu.roll(wa, LINES, 1) * a + pltpu.roll(wb, LINES, 1) * b
-            aux_into[half, k, m] = jnp.where(lane < LINES, high, total)
-            for g in range(HEADS):
-                tile = half * HEADS + g
-                into[half, k, m, g] = (
-                    spread(wa, tile) * pay[core, half, home, g].astype(F32)
-                    + spread(wb, tile) * epay[half, home, g].astype(F32)
-                ).astype(BF16)
+    def to_parts(x):
+        high = x.astype(BF16).astype(F32)
+        rest = x - high
+        mid = rest.astype(BF16).astype(F32)
+        top = jnp.where(lane < 2 * LINES, high, pltpu.roll(mid, 2 * LINES, 1))
+        return jnp.concatenate([top, rest - mid], axis=0).astype(BF16)
+
+    def from_parts(tile):
+        tile = tile.astype(F32)
+        top, low = tile[:REQ], tile[REQ:]
+        return (top + pltpu.roll(top, 2 * LINES, 1)) + low
+
+    def join(half, k, m, into):
+        home = chip ^ (k * 4 + m if half == 0 else m * 4 + k)
+        a, b = aux[core, home], eaux[home]
+        high = jnp.maximum(a, b)
+        wa, wb = jnp.exp(a - high), jnp.exp(b - high)
+        total = pltpu.roll(wa, LINES, 1) * a + pltpu.roll(wb, LINES, 1) * b
+        into[half, m, k, HEADS] = to_parts(jnp.where(lane < LINES, high, total))
+        for g in range(HEADS):
+            tile = half * HEADS + g
+            into[half, m, k, g] = (
+                spread(wa, tile) * pay[core, half, home, g].astype(F32)
+                + spread(wb, tile) * epay[half, home, g].astype(F32)
+            ).astype(BF16)
 
     def step_of(half, k):
         return me ^ (k * 8 if half == 0 else k * 2)
 
-    def first_pay(half, k):
-        at = half * 4 + k
+    def first_pay(half, m, k):
+        at = (half * 4 + m) * 4 + k
         return remote(
-            cpay.at[half, k], rpay.at[half, k], p_s.at[at], p_r.at[at], step_of(half, k), tp
-        )
-
-    def first_aux(half, k):
-        at = half * 4 + k
-        return remote(
-            caux.at[half, k], raux.at[half, k], a_s.at[at], a_r.at[at], step_of(half, k), tp
+            cpay.at[half, m, k], rpay.at[half, m, k], p_s.at[at], p_r.at[at], step_of(half, k), tp
         )
 
     def second_pay(half, m):
@@ -391,59 +390,77 @@
             spay.at[half, m], fpay.at[half, m], fp_s.at[at], fp_r.at[at], step_of(1 - half, m), tp
         )
 
-    def second_aux(half, m):
-        at = half * 4 + m
-        return remote(
-            saux.at[half, m], faux.at[half, m], fa_s.at[at], fa_r.at[at], step_of(1 - half, m), tp
-        )
-
-    def merge(half, m, into, aux_into):
-        parts = [raux[half, k, m] for k in range(4)]
+    def merge(half, m, into):
+        parts = [from_parts(rpay[half, m, k, HEADS]) for k in range(4)]
         high = functools.reduce(jnp.maximum, parts)
         weights = [jnp.exp(part - high) for part in parts]
         total = sum(pltpu.roll(wt, LINES, 1) * part for wt, part in zip(weights, parts))
-        aux_into[half, m] = jnp.where(lane < LINES, high, total)
+        into[half, m, HEADS] = to_parts(jnp.where(lane < LINES, high, total))
         for g in range(HEADS):
             tile = half * HEADS + g
             into[half, m, g] = sum(
-                spread(weights[k], tile) * rpay[half, k, m, g].astype(F32) for k in range(4)
+                spread(weights[k], tile) * rpay[half, m, k, g].astype(F32) for k in range(4)
             ).astype(BF16)
 
-    aux_join.start()
     owner_row = lax.fori_loop(0, SLOTS, owner_step, jnp.zeros((1, SLOTS), I32))
     for half in range(2):
         sum_slots(1 - core, half, owner_row)
         join_cores(half).start()
+    migrate_batch(2)
+
+    reqsum[...] = jnp.zeros(reqsum.shape, F32)
+
+    @pl.loop(0, GROUPS // 4)
+    def _(s):
+        total = reqsum[...]
+        for g in [s * 4 + i for i in range(4)]:
+            total += jnp.where(request == owners(g), ssum[pl.ds(g, 1), :], 0.0)
+        reqsum[...] = total
+
+    reqsum[...] = all_groups(reqsum[...], jnp.add)
+    aux[...] = jnp.where(lane < LINES, reqmax[...], reqsum[...]).reshape(aux.shape)
+    aux_join.start()
     for half in range(2):
         sum_slots(core, half, owner_row)
     aux_join.wait()
     join_cores(0).wait()
-    join_cores(1).wait()
-
-    for k in (2, 1, 3):
+
+    for m in (2, 1, 3, 0):
         for half in range(2):
-            join(half, k, cpay, caux)
-            first_aux(half, k).start()
-            first_pay(half, k).start()
+            if m == 2 and half == 1:
+                join_cores(1).wait()
+
+            @pl.loop(1, 4)
+            def _(k):
+                join(half, k, m, cpay)
+                first_pay(half, m, k).start()
+
+        if m == 1:
+            migrate_batch(3)
+
     for half in range(2):
-        join(half, 0, rpay, raux)
-    for k in (1, 3, 2):
+        pl.loop(0, 4)(lambda m: join(half, 0, m, rpay))
+
+    for m in (2, 1, 3, 0):
         for half in range(2):
-            first_aux(half, k).wait_recv()
-            first_pay(half, k).wait_recv()
-    for m in (2, 1, 3):
-        for half in range(2):
-            merge(half, m, spay, saux)
-            second_aux(half, m).start()
-            second_pay(half, m).start()
-    for half in range(2):
-        merge(half, 0, fpay, faux)
+            for k in (1, 3, 2):
+                first_pay(half, m, k).wait_recv()
+            merge(half, m, fpay if m == 0 else spay)
+            if m != 0:
+                second_pay(half, m).start()
+    migrate_batch(4)
+
     for half in range(2):
         for m in (1, 3, 2):
-            second_aux(half, m).wait_recv()
+            second_pay(half, m).wait_recv()
 
     parts = [
-        jnp.where(lane % LINES < LINES // 2, faux[0, m], faux[1, m]) for m in range(4)
+        jnp.where(
+            lane % LINES < LINES // 2,
+            from_parts(fpay[0, m, HEADS]),
+            from_parts(fpay[1, m, HEADS]),
+        )
+        for m in range(4)
     ]
     peak = functools.reduce(jnp.maximum, parts, dmax[...])
     weights = [jnp.exp(part - peak) for part in parts]
@@ -463,9 +480,6 @@
             ],
             axis=0,
         )
-    for half in range(2):
-        for m in (1, 3, 2):
-            second_pay(half, m).wait_recv()
     for tile in range(TILES):
         half, g = tile // HEADS, tile % HEADS
         line = acc[tile] + sum(
@@ -473,9 +487,7 @@
         )
         att[half * 16 : (half + 1) * 16, g * DIM : (g + 1) * DIM] = line.astype(BF16)
 
-    @pl.loop(1 + EARLY, INSTS)
-    def _(i):
-        migrate(i).start()
+    migrate_batch(5)
 
     w_load.wait()
 
@@ -514,16 +526,41 @@
                 gather_on(a, b, h).wait_send()
     own.wait()
     for half in range(2):
-        for k in range(1, 4):
-            first_aux(half, k).wait_send()
-            first_pay(half, k).wait_send()
-            second_aux(half, k).wait_send()
-            second_pay(half, k).wait_send()
+        for m in range(4):
+            for k in range(1, 4):
+                first_pay(half, m, k).wait_send()
+            if m != 0:
+                second_pay(half, m).wait_send()
     for k in range(1, TPS):
         send_columns(k).wait_send()
     @pl.loop(1, INSTS)
     def _(i):
         migrate(i).wait()
+
+
+def finish(out_hbm, moved_hbm, out, moved, out_held, held, in_sem, out_sem):
+    size = SLOTS // PARTS
+
+    def pair(i):
+        if i == PARTS:
+            return (
+                pltpu.make_async_copy(out_hbm, out_held, in_sem.at[i]),
+                pltpu.make_async_copy(out_held, out, out_sem.at[i]),
+            )
+        part = pl.ds(i * size, size)
+        return (
+            pltpu.make_async_copy(moved_hbm.at[part], held.at[part], in_sem.at[i]),
+            pltpu.make_async_copy(held.at[part], moved.at[part], out_sem.at[i]),
+        )
+
+    pairs = [pair(i) for i in range(PARTS + 1)]
+    for load, _ in pairs:
+        load.start()
+    for load, store in pairs:
+        load.wait()
+        store.start()
+    for _, store in pairs:
+        store.wait()
 
 
 def shards(queries, new_kv, kv_cache, block_owner, block_fill, move_slot, move_target, out_weight):
@@ -565,14 +602,10 @@
             pltpu.VMEM((2, CHIPS, REQ, DIM), F32),
             pltpu.VMEM((2, CHIPS, HEADS, 16, DIM), BF16),
             pltpu.VMEM((CHIPS, REQ, DIM), F32),
-            pltpu.VMEM((2, 4, 4, HEADS, 16, DIM), BF16),
-            pltpu.VMEM((2, 4, 4, REQ, DIM), F32),
-            pltpu.VMEM((2, 4, 4, HEADS, 16, DIM), BF16),
-            pltpu.VMEM((2, 4, 4, REQ, DIM), F32),
-            pltpu.VMEM((2, 4, HEADS, 16, DIM), BF16),
-            pltpu.VMEM((2, 4, REQ, DIM), F32),
-            pltpu.VMEM((2, 4, HEADS, 16, DIM), BF16),
-            pltpu.VMEM((2, 4, REQ, DIM), F32),
+            pltpu.VMEM((2, 4, 4, HEADS + 1, 16, DIM), BF16),
+            pltpu.VMEM((2, 4, 4, HEADS + 1, 16, DIM), BF16),
+            pltpu.VMEM((2, 4, HEADS + 1, 16, DIM), BF16),
+            pltpu.VMEM((2, 4, HEADS + 1, 16, DIM), BF16),
             pltpu.VMEM((TILES, 16, DIM), F32),
             pltpu.VMEM((DRAFTS * REQ, HEADS * DIM), BF16),
             pltpu.VMEM((TPS, DRAFTS * REQ, COLS), BF16),
@@ -581,8 +614,7 @@
             dma((9,)), dma,
             dma((2 * CHIPS,)), dma((2 * CHIPS,)), dma((2 * CHIPS,)), dma((2 * CHIPS,)),
             dma((INSTS,)), dma((INSTS,)), dma((3,)), dma((3,)),
-            dma((8,)), dma((8,)), dma((8,)), dma((8,)),
-            dma((8,)), dma((8,)), dma((8,)), dma((8,)),
+            dma((32,)), dma((32,)), dma((8,)), dma((8,)),
             dma((TPS,)), dma((TPS,)),
         ],
         compiler_params=pltpu.CompilerParams(
@@ -599,6 +631,23 @@
         move_target.reshape(MOVES),
         out_weight,
     )
+    out, moved = pl.pallas_call(
+        finish,
+        out_shape=(
+            jax.ShapeDtypeStruct(out.shape, BF16),
+            jax.ShapeDtypeStruct(moved.shape, BF16),
+        ),
+        in_specs=[anywhere] * 2,
+        out_specs=(anywhere,) * 2,
+        scratch_shapes=[
+            pltpu.VMEM(out.shape, BF16),
+            pltpu.VMEM(moved.shape, BF16),
+            dma((PARTS + 1,)),
+            dma((PARTS + 1,)),
+        ],
+        compiler_params=pltpu.CompilerParams(vmem_limit_bytes=63 << 20),
+        name="finish",
+    )(out, moved)
     return out, moved.reshape(kv_cache.shape)
 
 

time: 75.6 us -> 63.2 us (0.84)
  Pallas kernels: 70.2 us -> 62.4 us
  local copies, waits for them, and re-layouts: 4.6 us -> 0 us
    pallas_call x1, Pallas kernels: 70.2 us -> 60 us  [shards(): pl.pallas_call(kernel, out_shape=(jax.ShapeDtypeStruct((DRAFTS * REQ, COL...]
    unnamed x2 -> x0, local copies, waits for them, and re-layouts: 4.6 us -> none
    pallas_call x0 -> x1, Pallas kernels: none -> 2.41 us  [shards(): pl.pallas_call(finish, out_shape=(jax.ShapeDtypeStruct(out.shape, BF16),...]
where the time goes in v3:
time: 63.2 us; the launch traced here: 63.1 us
  Pallas kernels  62.4 us (99%)
  between operations  0.64 us (1%)
    pallas_call x1, Pallas kernels, shards(): pl.pallas_call(kernel, out_shape=(jax.ShapeDtypeStruct((DRAFTS * REQ, COL...  60 us
    pallas_call x1, Pallas kernels, shards(): pl.pallas_call(finish, out_shape=(jax.ShapeDtypeStruct(out.shape, BF16),...  2.41 us

profile of v3, /device:TPU:1, one launch (start us, length us, event | category | flops | bytes accessed | tf_op | source)
XLA Modules:
  0.0 63.1 jit_solution(1890927639546206696)
XLA Ops:
  0.6 60.0 %decode.1 = (bf16[32,512]{1,0:T(8,128)(2,1)}, bf16[64,2,64,128]{3,2,1,0:T(8,128)(2,1)}) custom-call(bf16[8,32,128]{2,1,0:T(8,128)(2,1)} %bitcast.8, bf16[8,2,4,128]{3,2,1,0:T(4,128)(2,1)} %bitcast.9, bf16[64,2,64,128]{3,2,1,0:T(8,128)(2,1)} %bitcast.7, s32[64]{0:T(128)} %owner_hbm.1, s32[64]{0:T(128)} %fill_hbm.1, s32[24]{0:T(128)} %slot_hbm.1, s32[24]{0:T(128)} %bitcast.10, ...), custom_call_target="tpu_custom_call" | custom-call | tf_op jit(solution)/shard_map/decode/pallas_call | solution.py:570
  60.7 2.4 %finish.1 = (bf16[32,512]{1,0:T(8,128)(2,1)}, bf16[64,2,64,128]{3,2,1,0:T(8,128)(2,1)}) custom-call(bf16[32,512]{1,0:T(8,128)(2,1)} %get-tuple-element.6.out_hbm, bf16[64,2,64,128]{3,2,1,0:T(8,128)(2,1)} %get-tuple-element.7.moved_hbm), custom_call_target="tpu_custom_call" | custom-call | tf_op jit(solution)/shard_map/finish/pallas_call | solution.py:634

commit v4 on v3

--- a/solution.py
+++ b/solution.py
@@ -27,7 +27,8 @@
 TILES = LINES // 2
 COLS = 512
 MOVES = 24
-BATCHES = (8, 10, 2, 0, 4)
+BATCHES = (8, 10, 2, 0, 8)
+MULT = 27
 WIDE = 4
 PARTS = 8
 SUMS = 4
@@ -177,7 +178,7 @@
         return remote(ref, ref, sib_s.at[at], sib_r.at[at], sibling, tp)
 
     def migrate(i):
-        k = lax.rem(i * 11, INSTS)
+        k = lax.rem(i * MULT, INSTS)
         return remote(
             msend.at[pl.ds(CAPACITY * (me ^ k), CAPACITY)],
             moved.at[pl.ds(CAPACITY * me, CAPACITY)],

time: 63.2 us -> 61.8 us (0.978)
  Pallas kernels: 62.4 us -> 60.5 us
    pallas_call x1, Pallas kernels: 60 us -> 58 us  [shards(): pl.pallas_call(kernel, out_shape=(jax.ShapeDtypeStruct((DRAFTS * REQ, COL...]
where the time goes in v4:
time: 61.8 us; the launch traced here: 61.1 us
  Pallas kernels  60.5 us (98%)
  between operations  0.64 us (1%)
    pallas_call x1, Pallas kernels, shards(): pl.pallas_call(kernel, out_shape=(jax.ShapeDtypeStruct((DRAFTS * REQ, COL...  58 us
    pallas_call x1, Pallas kernels, shards(): pl.pallas_call(finish, out_shape=(jax.ShapeDtypeStruct(out.shape, BF16),...  2.41 us

profile of v4, /device:TPU:1, one launch (start us, length us, event | category | flops | bytes accessed | tf_op | source)
XLA Modules:
  0.0 61.1 jit_solution(16738054781913128406)
XLA Ops:
  0.6 58.0 %decode.1 = (bf16[32,512]{1,0:T(8,128)(2,1)}, bf16[64,2,64,128]{3,2,1,0:T(8,128)(2,1)}) custom-call(bf16[8,32,128]{2,1,0:T(8,128)(2,1)} %bitcast.8, bf16[8,2,4,128]{3,2,1,0:T(4,128)(2,1)} %bitcast.9, bf16[64,2,64,128]{3,2,1,0:T(8,128)(2,1)} %bitcast.7, s32[64]{0:T(128)} %owner_hbm.1, s32[64]{0:T(128)} %fill_hbm.1, s32[24]{0:T(128)} %slot_hbm.1, s32[24]{0:T(128)} %bitcast.10, ...), custom_call_target="tpu_custom_call" | custom-call | tf_op jit(solution)/shard_map/decode/pallas_call | solution.py:571
  58.7 2.4 %finish.1 = (bf16[32,512]{1,0:T(8,128)(2,1)}, bf16[64,2,64,128]{3,2,1,0:T(8,128)(2,1)}) custom-call(bf16[32,512]{1,0:T(8,128)(2,1)} %get-tuple-element.6.out_hbm, bf16[64,2,64,128]{3,2,1,0:T(8,128)(2,1)} %get-tuple-element.7.moved_hbm), custom_call_target="tpu_custom_call" | custom-call | tf_op jit(solution)/shard_map/finish/pallas_call | solution.py:635

commit v5 on v4

--- a/solution.py
+++ b/solution.py
@@ -29,7 +29,7 @@
 MOVES = 24
 BATCHES = (8, 10, 2, 0, 8)
 MULT = 27
-WIDE = 4
+WIDE = 8
 PARTS = 8
 SUMS = 4
 
@@ -431,8 +431,9 @@
             if m == 2 and half == 1:
                 join_cores(1).wait()
 
-            @pl.loop(1, 4)
-            def _(k):
+            @pl.loop(0, 3)
+            def _(i):
+                k = lax.rem(i + 1, 3) + 1
                 join(half, k, m, cpay)
                 first_pay(half, m, k).start()
 

time: 61.8 us -> 61.9 us (level)
  no operation moved by 1% of the time
where the time goes in v5:
time: 61.9 us; the launch traced here: 61.1 us
  Pallas kernels  60.5 us (98%)
  between operations  0.64 us (1%)
    pallas_call x1, Pallas kernels, shards(): pl.pallas_call(kernel, out_shape=(jax.ShapeDtypeStruct((DRAFTS * REQ, COL...  58 us
    pallas_call x1, Pallas kernels, shards(): pl.pallas_call(finish, out_shape=(jax.ShapeDtypeStruct(out.shape, BF16),...  2.41 us

profile of v5, /device:TPU:1, one launch (start us, length us, event | category | flops | bytes accessed | tf_op | source)
XLA Modules:
  0.0 61.1 jit_solution(11399922305263077612)
XLA Ops:
  0.6 58.0 %decode.1 = (bf16[32,512]{1,0:T(8,128)(2,1)}, bf16[64,2,64,128]{3,2,1,0:T(8,128)(2,1)}) custom-call(bf16[8,32,128]{2,1,0:T(8,128)(2,1)} %bitcast.8, bf16[8,2,4,128]{3,2,1,0:T(4,128)(2,1)} %bitcast.9, bf16[64,2,64,128]{3,2,1,0:T(8,128)(2,1)} %bitcast.7, s32[64]{0:T(128)} %owner_hbm.1, s32[64]{0:T(128)} %fill_hbm.1, s32[24]{0:T(128)} %slot_hbm.1, s32[24]{0:T(128)} %bitcast.10, ...), custom_call_target="tpu_custom_call" | custom-call | tf_op jit(solution)/shard_map/decode/pallas_call | solution.py:572
  58.7 2.4 %finish.1 = (bf16[32,512]{1,0:T(8,128)(2,1)}, bf16[64,2,64,128]{3,2,1,0:T(8,128)(2,1)}) custom-call(bf16[32,512]{1,0:T(8,128)(2,1)} %get-tuple-element.6.out_hbm, bf16[64,2,64,128]{3,2,1,0:T(8,128)(2,1)} %get-tuple-element.7.moved_hbm), custom_call_target="tpu_custom_call" | custom-call | tf_op jit(solution)/shard_map/finish/pallas_call | solution.py:636
